TPU v7x, 1024 devices: a whole 4x8x16 slice. The times are simulated.
1024 devices in a mesh: node: 64 (over y, x, core), local: 16 (over z).
Axes of the slice: x: 4, y: 8, z: 16, core: 2. Of those that a mesh axis runs over, the one named last changes fastest.
Arguments:
- output_gradient: bfloat16 [8192, 3584], P(('node', 'local')), may hold values from -6 to 6
- expert_ids: int32 [8192, 8], P(('node', 'local')), may hold values from 0 to 127, as said below
- gate_weights: bfloat16 [8192, 8], P(('node', 'local')), may hold values from 0.099609375 to 0.59765625
- saved_gate: bfloat16 [524288, 128], P(('node', 'local')), may hold values from -6 to 6
- saved_up: bfloat16 [524288, 128], P(('node', 'local')), may hold values from -6 to 6
- w_gate: bfloat16 [1024, 3584, 128], P(('node', 'local')), may hold values from -0.375 to 0.375
- w_up: bfloat16 [1024, 3584, 128], P(('node', 'local')), may hold values from -0.375 to 0.375
- w_down: bfloat16 [1024, 128, 3584], P(('node', 'local')), may hold values from -0.0234375 to 0.0234375
Outputs:
- grad_in: bfloat16 [8192, 3584], P(('node', 'local'))
- grad_gate: bfloat16 [8192, 8], P(('node', 'local'))
Inputs may be any that keep to these rules, and one draw needn't show every extreme that they name: `expert_ids`: each token names 8 different experts, columns 2j and 2j+1 two experts of one node group (expert E lies in group E // 2), and its 4 groups differ. At most 1 token of one device name a given node group, and some group is named that often by every device. Over the tokens of all devices with one local index, at most 32 name a given expert, and in every draw some expert of some node group reaches that from every local index.
All inputs are finite; a program needn't handle non-finite values.
Results may differ from a plain program's by a relative error of at most 0.015.
Values may be sent and summed in bfloat16 or wider, within the bound.
No kernel may reach another device: no remote copies, remote signals or barrier semaphores. Data moves between devices by JAX's collectives and lax.ppermute only.
A program may use at most 32 MiB of HBM per device.

v0:
```python
import jax
import jax.numpy as jnp
from jax import lax
from jax.sharding import PartitionSpec as P

EXP_NODE = 2
TOPK = 8
NODES_TOK = 4


def expert_backward(rows, gate, saved_gate, saved_up, w_gate, w_up, w_down):
    flat_rows = rows.reshape(-1, rows.shape[-1])
    flat_gate = gate.reshape(-1).astype(jnp.float32)
    dims = (((1,), (1,)), ((), ()))
    upward = lax.dot_general(flat_rows, w_down[0], dims, preferred_element_type=jnp.float32)
    pre_gate = saved_gate.astype(jnp.float32)
    pre_up = saved_up.astype(jnp.float32)
    sigma = jax.nn.sigmoid(pre_gate)
    active = pre_gate * sigma
    gate_part = jnp.sum(active * pre_up * upward, axis=1).astype(jnp.bfloat16)
    scaled = flat_gate[:, None] * upward
    grad_gate_pre = (scaled * pre_up * sigma * (1.0 + pre_gate * (1.0 - sigma))).astype(
        jnp.bfloat16
    )
    grad_up_pre = (scaled * active).astype(jnp.bfloat16)
    back = lax.dot_general(grad_gate_pre, w_gate[0], dims, preferred_element_type=jnp.float32)
    back = back + lax.dot_general(grad_up_pre, w_up[0], dims, preferred_element_type=jnp.float32)
    return (back.astype(jnp.bfloat16).reshape(rows.shape), gate_part.reshape(gate.shape))


def on_device(
    output_gradient, expert_ids, gate_weights, saved_gate, saved_up, w_gate, w_up, w_down
):
    node_count = lax.axis_size("node")
    local_count = lax.axis_size("local")
    tok_count = output_gradient.shape[0]
    width = output_gradient.shape[1]
    route_count = tok_count * NODES_TOK
    capacity = (route_count + node_count - 1) // node_count
    receive_count = node_count * capacity
    shard_count = local_count // EXP_NODE
    pairs = expert_ids.reshape(tok_count, NODES_TOK, 2)
    dest_node = (pairs[:, :, 0] // EXP_NODE).reshape(route_count)
    local_exp = pairs % EXP_NODE
    node_hit = (dest_node[:, None] == jnp.arange(node_count, dtype=jnp.int32)[None, :]).astype(
        jnp.int32
    )
    slot = jnp.sum((jnp.cumsum(node_hit, axis=0) - node_hit) * node_hit, axis=1)
    target = dest_node * capacity + slot
    placing = (jnp.arange(receive_count, dtype=jnp.int32)[:, None] == target[None, :]).reshape(
        receive_count, tok_count, NODES_TOK
    )
    placing_float = placing.astype(jnp.float32)
    pick = jnp.sum(placing.astype(jnp.int32), axis=2).astype(jnp.bfloat16)
    outgoing_rows = jnp.dot(pick, output_gradient, preferred_element_type=jnp.float32).astype(
        jnp.bfloat16
    )
    expert_hit = (
        local_exp[:, :, :, None] == jnp.arange(EXP_NODE, dtype=jnp.int32)[None, None, None, :]
    ).astype(jnp.float32)
    route_gate = jnp.sum(
        expert_hit * gate_weights.reshape(tok_count, NODES_TOK, 2, 1).astype(jnp.float32), axis=2
    )
    send_gate = jnp.einsum(
        "qij,ije->qe", placing_float, route_gate, precision=lax.Precision.HIGHEST
    ).astype(jnp.bfloat16)
    rows_in, gates_in = (
        lax.all_to_all(
            outgoing_rows.reshape(node_count, capacity, width),
            "node",
            split_axis=0,
            concat_axis=0,
            tiled=True,
        ),
        lax.all_to_all(
            send_gate.reshape(node_count, capacity, EXP_NODE),
            "node",
            split_axis=0,
            concat_axis=0,
            tiled=True,
        ),
    )
    rows_in = rows_in.reshape(receive_count, width)
    gates_in = gates_in.reshape(receive_count, EXP_NODE)
    live = (gates_in > 0).astype(jnp.int32)
    rank = jnp.cumsum(live, axis=0) - live
    spot = (rank.T[:, None, :] == jnp.arange(route_count, dtype=jnp.int32)[None, :, None]) & (
        live.T[:, None, :] > 0
    )
    spread = spot.astype(jnp.bfloat16)
    owner = lax.axis_index("local") // shard_count
    portion_rows = lax.all_gather(rows_in, "local", axis=0, tiled=True)
    piece_gate = lax.all_gather(gates_in, "local", axis=0, tiled=True)
    blocks = portion_rows.shape[0] // receive_count
    portion_rows = portion_rows.reshape(blocks, receive_count, width)
    selector = (jnp.arange(EXP_NODE, dtype=jnp.int32) == owner).astype(jnp.float32)
    own_gate = jnp.sum(
        piece_gate.reshape(blocks, receive_count, EXP_NODE).astype(jnp.float32) * selector, axis=2
    )
    flag = (own_gate > 0).astype(jnp.int32)
    order = jnp.cumsum(flag, axis=1) - flag
    picked_experts = (
        order[:, None, :] == jnp.arange(route_count, dtype=jnp.int32)[None, :, None]
    ) & (flag[:, None, :] > 0)
    fresh_rows = jnp.einsum(
        "wrj,wja->wra",
        picked_experts.astype(jnp.bfloat16),
        portion_rows,
        preferred_element_type=jnp.float32,
    ).astype(jnp.bfloat16)
    new_gate = jnp.sum(picked_experts.astype(jnp.float32) * own_gate[:, None, :], axis=2).astype(
        jnp.bfloat16
    )
    returned_rows, gate_part = expert_backward(
        fresh_rows, new_gate, saved_gate, saved_up, w_gate, w_up, w_down
    )
    parts_back, gate_back = (
        lax.all_to_all(returned_rows, "local", split_axis=0, concat_axis=0, tiled=True),
        lax.all_to_all(gate_part, "local", split_axis=0, concat_axis=0, tiled=True),
    )
    parts_back = parts_back.reshape(EXP_NODE, shard_count, route_count, width)
    node_sum = jnp.einsum(
        "epq,espd->qd", spread, parts_back, preferred_element_type=jnp.float32
    ).astype(jnp.bfloat16)
    gate_sum = jnp.einsum(
        "epq,esp->qe",
        spot.astype(jnp.float32),
        gate_back.reshape(EXP_NODE, shard_count, route_count).astype(jnp.float32),
        precision=lax.Precision.HIGHEST,
    ).astype(jnp.bfloat16)
    rows_back, gates_home = (
        lax.all_to_all(
            node_sum.reshape(node_count, capacity, width),
            "node",
            split_axis=0,
            concat_axis=0,
            tiled=True,
        ),
        lax.all_to_all(
            gate_sum.reshape(node_count, capacity, EXP_NODE),
            "node",
            split_axis=0,
            concat_axis=0,
            tiled=True,
        ),
    )
    rows_back = rows_back.reshape(receive_count, width)
    grad_in = jnp.dot(pick.T, rows_back, preferred_element_type=jnp.float32).astype(jnp.bfloat16)
    per_pair = jnp.einsum(
        "qij,qe->ije",
        placing_float,
        gates_home.reshape(receive_count, EXP_NODE).astype(jnp.float32),
        precision=lax.Precision.HIGHEST,
    )
    grad_gate = (
        jnp.sum(per_pair[:, :, None, :] * expert_hit, axis=3)
        .reshape(tok_count, TOPK)
        .astype(jnp.bfloat16)
    )
    return (grad_in, grad_gate)


def solution(mesh):
    placed = (
        P(("node", "local"), None),
        P(("node", "local"), None),
        P(("node", "local"), None),
        P(("node", "local"), None),
        P(("node", "local"), None),
        P(("node", "local"), None, None),
        P(("node", "local"), None, None),
        P(("node", "local"), None, None),
    )
    return jax.shard_map(
        on_device,
        mesh=mesh,
        in_specs=placed,
        out_specs=(P(("node", "local"), None), P(("node", "local"), None)),
        check_vma=False,
    )
```

profile of v0, /device:TPU:1, one launch (start us, length us, event | category | flops | bytes accessed | tf_op | source)
XLA Modules:
  0.0 388.3 jit_solution(6918141577689017536)
XLA Ops:
  7.2 0.8 copy.100
  8.4 0.2 select_reduce_fusion.1
  8.8 1.1 fusion.1
  10.0 0.5 broadcast.180
  10.5 0.9 reduce.1
  11.4 0.1 reshape.258
  11.5 33.9 %all_to_all.31 = bf16[64,2,1792]{2,1,0:T(2,128)(2,1)S(1)} all-to-all(bf16[64,2,1792]{2,1,0:T(2,128)(2,1)S(1)} %reshape.258), channel_id=1, replica_groups=mesh['node'=64,'local'=16] {'node'}, dimensions={0} | all-to-all | bytes 917504 | tf_op jit(solution)/shard_map/all_to_all | solution.py:68
  45.4 0.4 reshape.259
  45.8 0.8 copy.113
  46.6 0.8 copy.126
  47.4 0.2 fusion.4
  47.6 0.7 copy.107
  48.4 5.7 %all-to-all-start = ((bf16[64,1,2]{2,1,0:T(2,128)(2,1)}), bf16[64,1,2]{2,1,0:T(2,128)(2,1)S(1)}, u32[]{:S(2)}, u32[]{:S(2)}) async-start(bf16[64,1,2]{2,1,0:T(2,128)(2,1)} %copy.107), calls=%async_computation | async-start | bytes 65536 | tf_op jit(solution)/shard_map/all_to_all | solution.py:75
  54.0 1.0 copy.115
  55.1 1.0 copy.114
  56.1 7.2 %all-to-all-done = bf16[64,1,2]{2,1,0:T(2,128)(2,1)S(1)} async-done(((bf16[64,1,2]{2,1,0:T(2,128)(2,1)}), bf16[64,1,2]{2,1,0:T(2,128)(2,1)S(1)}, u32[]{:S(2)}, u32[]{:S(2)}) %all-to-all-start) | async-done | bytes 288 | tf_op jit(solution)/shard_map/all_to_all | solution.py:75
  63.3 40.2 %all-gather = bf16[1024,1,2]{2,1,0:T(2,128)(2,1)S(1)} all-gather(bf16[64,1,2]{2,1,0:T(2,128)(2,1)S(1)} %all-to-all-done), channel_id=2, replica_groups=mesh['node'=64,'local'=16] {'local'}, dimensions={0}, use_global_device_ids=true | all-gather | bytes 4352 | tf_op jit(solution)/shard_map/all_gather | solution.py:93
  103.5 0.5 convert_element_type.181
  104.0 0.2 multiply_reduce_fusion
  104.3 0.2 reduce_window_sum.35
  104.5 0.2 select_reduce_fusion
  104.8 44.0 %all-gather.4.cloned.1.call-done = bf16[1024,1,3584]{2,0,1:T(8,128)(2,1)} async-done(((bf16[64,1,3584]{2,0,1:T(8,128)(2,1)}), bf16[1024,1,3584]{2,0,1:T(8,128)(2,1)}) %all-gather.4.cloned.1.call-update) | async-done | bytes 7340048 | tf_op jit(solution)/shard_map/all_gather | solution.py:92
  148.7 4.3 %convolution_convert_fusion = bf16[16,32,3584]{2,1,0:T(8,128)(2,1)S(1)} fusion(bf16[16,64,3584]{2,1,0:T(8,128)(2,1)} %bitcast.79, s32[16,64]{1,0:T(8,128)S(1)} %fusion.54, pred[16,64]{1,0:T(8,128)(4,1)S(1)} %get-tuple-element.14), kind=kOutput, calls=%fused_computation.2 | convolution fusion | flops 236781568 | bytes 11015168 | tf_op jit(solution)/shard_map/wrj,wja->wra/dot_general | solution.py:105
  153.1 1.3 fusion.16
  154.4 0.7 convert_element_type.183
  155.1 7.9 %all-to-all-start.4 = ((bf16[16,1,32]{2,1,0:T(2,128)(2,1)}), bf16[16,1,32]{2,1,0:T(2,128)(2,1)S(1)}, u32[]{:S(2)}, u32[]{:S(2)}) async-start(bf16[16,1,32]{2,1,0:T(2,128)(2,1)} %convert_element_type.183), calls=%async_computation.4 | async-start | bytes 16384 | tf_op jit(solution)/shard_map/all_to_all | solution.py:119
  163.0 1.2 fusion.6
  164.2 3.0 add_convert_fusion
  167.2 7.0 %all-to-all-done.4 = bf16[16,1,32]{2,1,0:T(2,128)(2,1)S(1)} async-done(((bf16[16,1,32]{2,1,0:T(2,128)(2,1)}), bf16[16,1,32]{2,1,0:T(2,128)(2,1)S(1)}, u32[]{:S(2)}, u32[]{:S(2)}) %all-to-all-start.4) | async-done | bytes 1056 | tf_op jit(solution)/shard_map/all_to_all | solution.py:119
  174.2 4.5 %all-to-all-start.2 = ((bf16[16,32,3584]{2,1,0:T(8,128)(2,1)}), bf16[16,32,3584]{2,1,0:T(8,128)(2,1)}, u32[]{:S(2)}, u32[]{:S(2)}) async-start(bf16[16,32,3584]{2,1,0:T(8,128)(2,1)} %bitcast.80), calls=%async_computation.2 | async-start | bytes 7340032 | tf_op jit(solution)/shard_map/all_to_all | solution.py:118
  178.7 0.1 copy.108
  178.8 0.1 copy.109
  178.9 0.1 reduce_window_sum.34
  179.1 0.1 fusion.30
  179.3 0.7 copy.118
  180.0 158.0 %all-to-all-done.2 = bf16[16,32,3584]{2,1,0:T(8,128)(2,1)} async-done(((bf16[16,32,3584]{2,1,0:T(8,128)(2,1)}), bf16[16,32,3584]{2,1,0:T(8,128)(2,1)}, u32[]{:S(2)}, u32[]{:S(2)}) %all-to-all-start.2) | async-done | bytes 3670048 | tf_op jit(solution)/shard_map/all_to_all | solution.py:118
  338.0 10.8 %all-to-all-start.5 = ((bf16[64,1,2]{2,1,0:T(2,128)(2,1)}), bf16[64,1,2]{2,1,0:T(2,128)(2,1)S(1)}, u32[]{:S(2)}, u32[]{:S(2)}) async-start(bf16[64,1,2]{2,1,0:T(2,128)(2,1)} %copy.118), calls=%async_computation.5 | async-start | bytes 65536 | tf_op jit(solution)/shard_map/all_to_all | solution.py:139
  348.9 2.5 convert_reduce_fusion
  351.4 0.3 fusion.2
  351.8 0.9 reduce.2
  352.7 0.9 reshape.260
  353.6 4.6 %all-to-all-done.5 = bf16[64,1,2]{2,1,0:T(2,128)(2,1)S(1)} async-done(((bf16[64,1,2]{2,1,0:T(2,128)(2,1)}), bf16[64,1,2]{2,1,0:T(2,128)(2,1)S(1)}, u32[]{:S(2)}, u32[]{:S(2)}) %all-to-all-start.5) | async-done | bytes 288 | tf_op jit(solution)/shard_map/all_to_all | solution.py:139
  358.2 5.7 %all-to-all-start.3 = ((bf16[64,2,1792]{2,1,0:T(2,128)(2,1)}), bf16[64,2,1792]{2,1,0:T(2,128)(2,1)S(1)}, u32[]{:S(2)}, u32[]{:S(2)}) async-start(bf16[64,2,1792]{2,1,0:T(2,128)(2,1)} %reshape.260), calls=%async_computation.3 | async-start | bytes 917504 | tf_op jit(solution)/shard_map/all_to_all | solution.py:132
  364.0 0.2 fusion.39
  364.2 0.7 copy.122
  364.9 15.4 %all-to-all-done.3 = bf16[64,2,1792]{2,1,0:T(2,128)(2,1)S(1)} async-done(((bf16[64,2,1792]{2,1,0:T(2,128)(2,1)}), bf16[64,2,1792]{2,1,0:T(2,128)(2,1)S(1)}, u32[]{:S(2)}, u32[]{:S(2)}) %all-to-all-start.3) | async-done | bytes 458784 | tf_op jit(solution)/shard_map/all_to_all | solution.py:132
  380.3 0.4 reshape.261
  380.6 0.8 convolution_convert_fusion.2
  (38 shorter events, 1.1 us)
Async XLA Ops:
  7.2 155.8 %copy-start = (bf16[1,3584,128]{2,1,0:T(8,128)(2,1)S(1)}, bf16[1,3584,128]{2,1,0:T(8,128)(2,1)}, u32[]{:S(2)}) copy-start(bf16[1,3584,128]{2,1,0:T(8,128)(2,1)} %param.13) | copy-start | bytes 2752516
  7.2 141.6 %all-gather.4.cloned.1.call-start = ((), (), s32[]{:S(2)}) async-start(), calls=%async_computation.6 | async-start | bytes 7798784 | tf_op jit(solution)/shard_map/all_gather | solution.py:92
  48.4 15.0 %all-to-all-start = ((bf16[64,1,2]{2,1,0:T(2,128)(2,1)}), bf16[64,1,2]{2,1,0:T(2,128)(2,1)S(1)}, u32[]{:S(2)}, u32[]{:S(2)}) async-start(bf16[64,1,2]{2,1,0:T(2,128)(2,1)} %copy.107), calls=%async_computation | async-start | bytes 65536 | tf_op jit(solution)/shard_map/all_to_all | solution.py:75
  148.7 4.3 %copy-start.2 = (bf16[1,128,3584]{2,1,0:T(8,128)(2,1)S(1)}, bf16[1,128,3584]{2,1,0:T(8,128)(2,1)}, u32[]{:S(2)}) copy-start(bf16[1,128,3584]{2,1,0:T(8,128)(2,1)} %param.15) | copy-start | bytes 2752516
  154.4 9.8 %copy-start.1 = (bf16[1,3584,128]{2,1,0:T(8,128)(2,1)S(1)}, bf16[1,3584,128]{2,1,0:T(8,128)(2,1)}, u32[]{:S(2)}) copy-start(bf16[1,3584,128]{2,1,0:T(8,128)(2,1)} %param.14) | copy-start | bytes 2752516
  155.1 19.1 %all-to-all-start.4 = ((bf16[16,1,32]{2,1,0:T(2,128)(2,1)}), bf16[16,1,32]{2,1,0:T(2,128)(2,1)S(1)}, u32[]{:S(2)}, u32[]{:S(2)}) async-start(bf16[16,1,32]{2,1,0:T(2,128)(2,1)} %convert_element_type.183), calls=%async_computation.4 | async-start | bytes 16384 | tf_op jit(solution)/shard_map/all_to_all | solution.py:119
  174.2 163.8 %all-to-all-start.2 = ((bf16[16,32,3584]{2,1,0:T(8,128)(2,1)}), bf16[16,32,3584]{2,1,0:T(8,128)(2,1)}, u32[]{:S(2)}, u32[]{:S(2)}) async-start(bf16[16,32,3584]{2,1,0:T(8,128)(2,1)} %bitcast.80), calls=%async_computation.2 | async-start | bytes 7340032 | tf_op jit(solution)/shard_map/all_to_all | solution.py:118
  338.0 20.2 %all-to-all-start.5 = ((bf16[64,1,2]{2,1,0:T(2,128)(2,1)}), bf16[64,1,2]{2,1,0:T(2,128)(2,1)S(1)}, u32[]{:S(2)}, u32[]{:S(2)}) async-start(bf16[64,1,2]{2,1,0:T(2,128)(2,1)} %copy.118), calls=%async_computation.5 | async-start | bytes 65536 | tf_op jit(solution)/shard_map/all_to_all | solution.py:139
  358.2 22.1 %all-to-all-start.3 = ((bf16[64,2,1792]{2,1,0:T(2,128)(2,1)}), bf16[64,2,1792]{2,1,0:T(2,128)(2,1)S(1)}, u32[]{:S(2)}, u32[]{:S(2)}) async-start(bf16[64,2,1792]{2,1,0:T(2,128)(2,1)} %reshape.260), calls=%async_computation.3 | async-start | bytes 917504 | tf_op jit(solution)/shard_map/all_to_all | solution.py:132
Sparse Core Ops, SparseCore 0:
  46.7 101.9 all-gather.3
where the time goes:
time: 389 us; the launch traced here: 388 us
  waiting for transfers between devices  236 us (61%)
  blocking collectives  74.1 us (19%)
  starting transfers between devices  34.6 us (9%)
  between operations  14.3 us (4%)
  matrix products  12.6 us (3%)
  local copies, waits for them, and re-layouts  10.3 us (3%)
  other arithmetic  6.15 us (2%)
    all_to_all x1, waiting for transfers between devices, on_device(): lax.all_to_all(returned_rows, 'local', split_axis=0, concat_axis=0, tiled...  158 us
    all_gather x1, waiting for transfers between devices, on_device(): portion_rows = lax.all_gather(rows_in, 'local', axis=0, tiled=True)  44 us
    all_gather x1, blocking collectives, on_device(): piece_gate = lax.all_gather(gates_in, 'local', axis=0, tiled=True)  40.2 us
    all_to_all x1, blocking collectives, on_device(): lax.all_to_all(outgoing_rows.reshape(node_count, capacity, width), 'node'...  33.9 us
    all_to_all x1, waiting for transfers between devices, on_device(): lax.all_to_all(node_sum.reshape(node_count, capacity, width), 'node', spl...  15.4 us
    all_to_all x1, starting transfers between devices, on_device(): lax.all_to_all(gate_sum.reshape(node_count, capacity, EXP_NODE), 'node',...  10.8 us
    all_to_all x1, starting transfers between devices, on_device(): lax.all_to_all(gate_part, 'local', split_axis=0, concat_axis=0, tiled=True)  7.88 us
  transfers between devices with their start and end apart: 6, of which 6 were waited for; matrix products, arithmetic and copies ran while one was open for 4% of the time, Pallas kernels for 0%

commit v1 on v0

v1 whole, which is shorter than its diff:
```python
import jax
import jax.numpy as jnp
from jax import lax
from jax.sharding import PartitionSpec as P

EXP_NODE = 2
TOPK = 8
NODES_TOK = 4
EXTRA = 128


def expert_backward(rows, gate, saved_gate, saved_up, w_gate, w_up, w_down):
    dims = (((1,), (1,)), ((), ()))
    upward = lax.dot_general(rows, w_down, dims, preferred_element_type=jnp.float32)
    pre_gate = saved_gate.astype(jnp.float32)
    pre_up = saved_up.astype(jnp.float32)
    sigma = jax.nn.sigmoid(pre_gate)
    active = pre_gate * sigma
    gate_part = jnp.sum(active * pre_up * upward, axis=1)
    scaled = gate[:, None] * upward
    grad_gate_pre = (scaled * pre_up * sigma * (1.0 + pre_gate * (1.0 - sigma))).astype(
        jnp.bfloat16
    )
    grad_up_pre = (scaled * active).astype(jnp.bfloat16)
    back = lax.dot_general(grad_gate_pre, w_gate, dims, preferred_element_type=jnp.float32)
    back = back + lax.dot_general(grad_up_pre, w_up, dims, preferred_element_type=jnp.float32)
    return back.astype(jnp.bfloat16), gate_part


def exchange(x):
    count, width = x.shape
    x = lax.all_to_all(
        x.reshape(count, 1, width), "node", split_axis=0, concat_axis=0, tiled=True
    )
    return x.reshape(count, width)


def on_device(
    output_gradient, expert_ids, gate_weights, saved_gate, saved_up, w_gate, w_up, w_down
):
    node_count = lax.axis_size("node")
    local_count = lax.axis_size("local")
    tok_count, width = output_gradient.shape
    live_count = tok_count * NODES_TOK
    shard_count = local_count // EXP_NODE
    owner = lax.axis_index("local") // shard_count

    pairs = expert_ids.reshape(tok_count, NODES_TOK, EXP_NODE)
    dest_node = pairs[:, :, 0] // EXP_NODE
    placing = jnp.arange(node_count, dtype=jnp.int32)[:, None, None] == dest_node[None]
    pick = jnp.any(placing, axis=2).astype(jnp.bfloat16)
    hit = (pairs % EXP_NODE)[..., None] == jnp.arange(EXP_NODE, dtype=jnp.int32)
    weights = gate_weights.reshape(tok_count, NODES_TOK, EXP_NODE, 1).astype(jnp.float32)
    route_gate = jnp.sum(jnp.where(hit, weights, 0.0), axis=2)
    send_gate = jnp.sum(jnp.where(placing[..., None], route_gate[None], 0.0), axis=(1, 2))
    send_rows = jnp.dot(pick, output_gradient, preferred_element_type=jnp.float32)
    send = jnp.concatenate(
        [
            send_rows.astype(jnp.bfloat16),
            send_gate.astype(jnp.bfloat16),
            jnp.zeros((node_count, EXTRA - EXP_NODE), jnp.bfloat16),
        ],
        axis=1,
    )
    slots = exchange(send)

    live = (slots[:, width] > 0).astype(jnp.int32)
    rank = jnp.cumsum(live) - live
    compact = (jnp.arange(live_count, dtype=jnp.int32)[:, None] == rank[None]) & (
        live[None] > 0
    )
    compact = compact.astype(jnp.bfloat16)
    rows = jnp.dot(compact, slots, preferred_element_type=jnp.float32).astype(jnp.bfloat16)
    rows = lax.all_gather(rows, "local", axis=0, tiled=True)

    gate = jnp.where(owner == 0, rows[:, width], rows[:, width + 1]).astype(jnp.float32)
    back, gate_part = expert_backward(
        rows[:, :width], gate, saved_gate, saved_up, w_gate[0], w_up[0], w_down[0]
    )
    column = lax.broadcasted_iota(jnp.int32, (back.shape[0], EXTRA), 1)
    extra = jnp.where(column == owner, gate_part[:, None], 0.0).astype(jnp.bfloat16)
    parts = jnp.concatenate([back, extra], axis=1)
    sums = lax.psum_scatter(parts, "local", scatter_dimension=0, tiled=True)

    home = exchange(
        lax.dot_general(
            compact, sums, (((0,), (0,)), ((), ())), preferred_element_type=jnp.float32
        ).astype(jnp.bfloat16)
    )
    grad_in = lax.dot_general(
        pick, home[:, :width], (((0,), (0,)), ((), ())), preferred_element_type=jnp.float32
    ).astype(jnp.bfloat16)
    gates_home = home[:, width : width + EXP_NODE].astype(jnp.float32)
    per_pair = jnp.sum(jnp.where(placing[..., None], gates_home[:, None, None, :], 0.0), axis=0)
    grad_gate = jnp.sum(jnp.where(hit, per_pair[:, :, None, :], 0.0), axis=3)
    return grad_in, grad_gate.reshape(tok_count, TOPK).astype(jnp.bfloat16)


def solution(mesh):
    placed = (
        P(("node", "local"), None),
        P(("node", "local"), None),
        P(("node", "local"), None),
        P(("node", "local"), None),
        P(("node", "local"), None),
        P(("node", "local"), None, None),
        P(("node", "local"), None, None),
        P(("node", "local"), None, None),
    )
    return jax.shard_map(
        on_device,
        mesh=mesh,
        in_specs=placed,
        out_specs=(P(("node", "local"), None), P(("node", "local"), None)),
        check_vma=False,
    )
```

time: 389 us -> 256 us (0.66)
  waiting for transfers between devices: 236 us -> 147 us
  starting transfers between devices: 34.6 us -> 0.08 us
  local copies, waits for them, and re-layouts: 10.3 us -> 5.81 us
    all_to_all x5 -> x0, waiting for transfers between devices: 192 us -> none  [the longest x1 158 us: on_device(): lax.all_to_all(returned_rows, 'local', split_axis=0, concat_axis=0, tiled...]
    reduce_scatter x0 -> x1, waiting for transfers between devices: none -> 77.6 us  [on_device(): sums = lax.psum_scatter(parts, 'local', scatter_dimension=0, tiled=True)]
    all_gather x1 -> x0, blocking collectives: 40.2 us -> none  [on_device(): piece_gate = lax.all_gather(gates_in, 'local', axis=0, tiled=True)]
    all_to_all x1 -> x2, blocking collectives: 33.9 us -> 72.2 us  [exchange(): lax.all_to_all(x.reshape(count, 1, width), 'node', split_axis=0, concat_a...]
    all_to_all x5 -> x0, starting transfers between devices: 34.6 us -> none  [the longest x1 10.8 us: on_device(): lax.all_to_all(gate_sum.reshape(node_count, capacity, EXP_NODE), 'node',...]
    all_gather x1, waiting for transfers between devices: 44 us -> 69.2 us  [on_device(): rows = lax.all_gather(rows, 'local', axis=0, tiled=True)]
    dot_general x9 -> x6, matrix products: 11.5 us -> 8.97 us  [the longest x1 3.6 us: expert_backward(): lax.dot_general(rows, w_down, dims, preferred_element_type=jnp.float32)]
  transfers between devices with their start and end apart: 6 -> 2, of which waited for: 6 -> 2; matrix products, arithmetic and copies ran while one was open for 4% -> 0% of each run, Pallas kernels for 0% -> 0%
where the time goes in v1:
time: 256 us; the launch traced here: 255 us
  waiting for transfers between devices  147 us (57%)
  blocking collectives  72.2 us (28%)
  between operations  14.3 us (6%)
  matrix products  10.1 us (4%)
  other arithmetic  5.91 us (2%)
  local copies, waits for them, and re-layouts  5.81 us (2%)
    reduce_scatter x1, waiting for transfers between devices, on_device(): sums = lax.psum_scatter(parts, 'local', scatter_dimension=0, tiled=True)  77.6 us
    all_to_all x2, blocking collectives, exchange(): lax.all_to_all(x.reshape(count, 1, width), 'node', split_axis=0, concat_a...  72.2 us
    all_gather x1, waiting for transfers between devices, on_device(): rows = lax.all_gather(rows, 'local', axis=0, tiled=True)  69.2 us
  transfers between devices with their start and end apart: 2, of which 2 were waited for; matrix products, arithmetic and copies ran while one was open for 0% of the time, Pallas kernels for 0%

profile of v1, /device:TPU:1, one launch (start us, length us, event | category | flops | bytes accessed | tf_op | source)
XLA Modules:
  0.0 255.2 jit_solution(8685999911067838855)
XLA Ops:
  7.2 0.0 copy-start
  7.2 0.0 all-gather.2.cloned.1.call-start
  7.2 0.8 copy.60
  8.1 0.1 iota_compare_fusion.1
  8.2 0.8 copy.78
  9.0 0.1 select_reduce_fusion.1
  9.0 0.1 copy.65
  9.2 1.1 convolution_convert_fusion
  10.3 0.0 copy-start.2
  10.3 0.1 concatenate.6
  10.4 0.0 copy-start.3
  10.5 0.5 broadcast.108
  11.0 0.9 reduce.6
  11.9 0.4 reshape.136
  12.3 34.6 %all_to_all.10 = bf16[64,2,1856]{2,1,0:T(2,128)(2,1)S(1)} all-to-all(bf16[64,2,1856]{2,1,0:T(2,128)(2,1)S(1)} %reshape.136), channel_id=1, replica_groups=mesh['node'=64,'local'=16] {'node'}, dimensions={0} | all-to-all | bytes 950272 | tf_op jit(solution)/shard_map/all_to_all | solution.py:32
  46.8 0.8 reshape.137
  47.6 0.1 copy.82
  47.7 0.1 compare_reduce_fusion
  47.8 0.1 reduce-window.8
  47.9 0.1 subtract_reduce_fusion
  48.0 0.9 convolution_convert_fusion.2
  48.9 0.0 all-gather.2.cloned.1.call-update
  49.0 0.0 reduce-scatter.2.cloned.1.call-start
  49.0 0.0 copy-done.2
  49.0 0.1 copy.68
  49.2 0.1 copy.67
  49.3 69.2 %all-gather.2.cloned.1.call-done = bf16[512,3712]{1,0:T(8,128)(2,1)} async-done(((bf16[32,3712]{1,0:T(8,128)(2,1)}), bf16[512,3712]{1,0:T(8,128)(2,1)}) %all-gather.2.cloned.1.call-update) | async-done | bytes 3801104 | tf_op jit(solution)/shard_map/all_gather | solution.py:74
  118.5 1.2 convert_reduce_fusion
  119.7 3.6 %fusion.12 = (bf16[512]{0:T(512)(128)(2,1)S(1)}, f32[512,128]{0,1:T(8,128)S(1)}) fusion(bf16[512,128]{0,1:T(8,128)(2,1)S(1)} %copy.67, bf16[512,128]{0,1:T(8,128)(2,1)S(1)} %copy.68, bf16[1,128,3584]{2,1,0:T(8,128)(2,1)} %param.15, bf16[512,3712]{1,0:T(8,128)(2,1)} %all-gather.2.cloned.1.call-done), kind=kOutput, calls=%fused_computation.25 | convolution fusion | flops 470351360 | bytes 5112832 | tf_op jit(solution)/shard_map/dot_general | solution.py:14
  123.3 0.0 copy-done
  123.3 0.0 copy-start.1
  123.3 1.2 fusion.4
  124.5 0.0 copy-done.1
  124.6 1.2 add_convert_fusion
  125.8 0.1 select_convert_fusion
  125.9 2.1 pad_maximum_fusion
  128.0 0.0 reduce-scatter.2.cloned.1.call-update
  128.0 77.6 %reduce-scatter.2.cloned.1.call-done = bf16[32,3712]{1,0:T(8,128)(2,1)} async-done(((bf16[512,3712]{1,0:T(8,128)(2,1)}), bf16[32,3712]{1,0:T(8,128)(2,1)}) %reduce-scatter.2.cloned.1.call-update) | async-done | bytes 237584 | tf_op jit(solution)/shard_map/reduce_scatter | solution.py:83
  205.6 1.3 fusion
  206.9 0.9 reduce.7
  207.8 0.4 reshape.138
  208.2 37.6 %all_to_all.11 = bf16[64,2,1856]{2,1,0:T(2,128)(2,1)S(1)} all-to-all(bf16[64,2,1856]{2,1,0:T(2,128)(2,1)S(1)} %reshape.138), channel_id=1, replica_groups=mesh['node'=64,'local'=16] {'node'}, dimensions={0} | all-to-all | bytes 950272 | tf_op jit(solution)/shard_map/all_to_all | solution.py:32
  245.8 0.8 reshape.139
  246.6 0.1 copy.81
  246.7 0.8 convolution_convert_fusion.3
  247.5 0.1 copy.76
  247.6 0.1 select_reduce_fusion
  247.7 0.7 copy.73
  (15 shorter events, 0.1 us)
Async XLA Ops:
  7.2 116.2 %copy-start = (bf16[1,3584,128]{2,1,0:T(8,128)(2,1)S(1)}, bf16[1,3584,128]{2,1,0:T(8,128)(2,1)}, u32[]{:S(2)}) copy-start(bf16[1,3584,128]{2,1,0:T(8,128)(2,1)} %param.13) | copy-start | bytes 2752516
  7.2 111.4 %all-gather.2.cloned.1.call-start = ((), (), s32[]{:S(2)}) async-start(), calls=%async_computation.3 | async-start | bytes 4038656 | tf_op jit(solution)/shard_map/all_gather | solution.py:74
  10.3 38.7 %copy-start.2 = (bf16[512,128]{1,0:T(8,128)(2,1)S(1)}, bf16[512,128]{1,0:T(8,128)(2,1)}, u32[]{:S(2)}) copy-start(bf16[512,128]{1,0:T(8,128)(2,1)} %param.11) | copy-start | bytes 393220
  10.4 38.7 %copy-start.3 = (bf16[512,128]{1,0:T(8,128)(2,1)S(1)}, bf16[512,128]{1,0:T(8,128)(2,1)}, u32[]{:S(2)}) copy-start(bf16[512,128]{1,0:T(8,128)(2,1)} %param.12) | copy-start | bytes 393220
  49.0 156.6 %reduce-scatter.2.cloned.1.call-start = ((), (), s32[]{:S(2)}) async-start(), calls=%async_computation.4 | async-start | bytes 4038656 | tf_op jit(solution)/shard_map/reduce_scatter | solution.py:83
  123.3 1.2 copy-start.1
Sparse Core Ops, SparseCore 0:
  49.1 69.3 all-gather.1
  128.1 77.4 reduce-scatter.1

commit v2 on v1

--- a/solution.py
+++ b/solution.py
@@ -1,6 +1,8 @@
 import jax
 import jax.numpy as jnp
 from jax import lax
+from jax.experimental import pallas as pl
+from jax.experimental.pallas import tpu as pltpu
 from jax.sharding import PartitionSpec as P
 
 EXP_NODE = 2
@@ -9,22 +11,71 @@
 EXTRA = 128
 
 
-def expert_backward(rows, gate, saved_gate, saved_up, w_gate, w_up, w_down):
-    dims = (((1,), (1,)), ((), ()))
-    upward = lax.dot_general(rows, w_down, dims, preferred_element_type=jnp.float32)
-    pre_gate = saved_gate.astype(jnp.float32)
-    pre_up = saved_up.astype(jnp.float32)
+def hidden_kernel(owner_ref, up_ref, extra_ref, sgate_ref, sup_ref, wg_ref, wu_ref, out_ref):
+    owner = owner_ref[0]
+    extra = extra_ref[...]
+    column = lax.broadcasted_iota(jnp.int32, extra.shape, 1)
+    gate = jnp.sum(jnp.where(column == owner, extra, 0.0), axis=1, keepdims=True)
+    shift = jnp.sum(jnp.where(column == EXP_NODE, extra, 0.0), axis=1, keepdims=True)
+    upward = up_ref[...] * jnp.exp2(-shift)
+    pre_gate = sgate_ref[...].astype(jnp.float32)
+    pre_up = sup_ref[...].astype(jnp.float32)
     sigma = jax.nn.sigmoid(pre_gate)
     active = pre_gate * sigma
-    gate_part = jnp.sum(active * pre_up * upward, axis=1)
-    scaled = gate[:, None] * upward
-    grad_gate_pre = (scaled * pre_up * sigma * (1.0 + pre_gate * (1.0 - sigma))).astype(
-        jnp.bfloat16
-    )
-    grad_up_pre = (scaled * active).astype(jnp.bfloat16)
-    back = lax.dot_general(grad_gate_pre, w_gate, dims, preferred_element_type=jnp.float32)
-    back = back + lax.dot_general(grad_up_pre, w_up, dims, preferred_element_type=jnp.float32)
-    return back.astype(jnp.bfloat16), gate_part
+    gate_part = jnp.sum(active * pre_up * upward, axis=1, keepdims=True)
+    scaled = gate * upward
+    grad_gate = (scaled * pre_up * sigma * (1.0 + pre_gate * (1.0 - sigma))).astype(jnp.bfloat16)
+    grad_up = (scaled * active).astype(jnp.bfloat16)
+    dims = (((1,), (1,)), ((), ()))
+    width = wg_ref.shape[0]
+    step = width // 7 if width % 896 == 0 else width
+    for start in range(0, width, step):
+        cols = slice(start, start + step)
+        back = lax.dot_general(grad_gate, wg_ref[cols, :], dims, preferred_element_type=jnp.float32)
+        back += lax.dot_general(grad_up, wu_ref[cols, :], dims, preferred_element_type=jnp.float32)
+        out_ref[:, cols] = back.astype(jnp.bfloat16)
+    out_ref[:, width:] = jnp.where(column == owner, gate_part, 0.0).astype(jnp.bfloat16)
+
+
+def hidden_parts(owner, upward, extra, saved_gate, saved_up, w_gate, w_up):
+    rows, hidden = upward.shape
+    width = w_gate.shape[0]
+    block = 128 if rows % 128 == 0 else rows
+    by_rows = lambda cols: pl.BlockSpec((block, cols), lambda i: (i, 0))
+    whole = lambda shape: pl.BlockSpec(shape, lambda i: (0, 0))
+    return pl.pallas_call(
+        hidden_kernel,
+        grid=(rows // block,),
+        in_specs=[
+            pl.BlockSpec(memory_space=pltpu.SMEM),
+            by_rows(hidden),
+            by_rows(EXTRA),
+            by_rows(hidden),
+            by_rows(hidden),
+            whole((width, hidden)),
+            whole((width, hidden)),
+        ],
+        out_specs=by_rows(width + EXTRA),
+        out_shape=jax.ShapeDtypeStruct((rows, width + EXTRA), jnp.bfloat16),
+        compiler_params=pltpu.CompilerParams(vmem_limit_bytes=24 * 2**20),
+        cost_estimate=pl.CostEstimate(
+            flops=4 * rows * width * hidden,
+            bytes_accessed=4 * width * hidden + 2 * rows * width,
+            transcendentals=rows * hidden,
+        ),
+    )(owner.reshape(1), upward, extra, saved_gate, saved_up, w_gate, w_up)
+
+
+def power_scale(rows):
+    largest = jnp.max(jnp.abs(rows.astype(jnp.float32)), axis=1, keepdims=True)
+    scale = jnp.ones_like(largest)
+    shift = jnp.zeros_like(largest)
+    for bits in (64, 32, 16, 8, 4, 2):
+        more = largest * 2.0**bits < 2.0**15
+        largest = jnp.where(more, largest * 2.0**bits, largest)
+        scale = jnp.where(more, scale * 2.0**bits, scale)
+        shift = jnp.where(more, shift + bits, shift)
+    return scale, shift
 
 
 def exchange(x):
@@ -53,12 +104,16 @@
     weights = gate_weights.reshape(tok_count, NODES_TOK, EXP_NODE, 1).astype(jnp.float32)
     route_gate = jnp.sum(jnp.where(hit, weights, 0.0), axis=2)
     send_gate = jnp.sum(jnp.where(placing[..., None], route_gate[None], 0.0), axis=(1, 2))
-    send_rows = jnp.dot(pick, output_gradient, preferred_element_type=jnp.float32)
+    scale, shift = power_scale(output_gradient)
+    scaled = (output_gradient.astype(jnp.float32) * scale).astype(jnp.bfloat16)
+    send_rows = jnp.dot(pick, scaled, preferred_element_type=jnp.float32)
+    send_shift = jnp.dot(pick, shift.astype(jnp.bfloat16), preferred_element_type=jnp.float32)
     send = jnp.concatenate(
         [
             send_rows.astype(jnp.bfloat16),
             send_gate.astype(jnp.bfloat16),
-            jnp.zeros((node_count, EXTRA - EXP_NODE), jnp.bfloat16),
+            send_shift.astype(jnp.bfloat16),
+            jnp.zeros((node_count, EXTRA - EXP_NODE - 1), jnp.bfloat16),
         ],
         axis=1,
     )
@@ -70,16 +125,19 @@
         live[None] > 0
     )
     compact = compact.astype(jnp.bfloat16)
-    rows = jnp.dot(compact, slots, preferred_element_type=jnp.float32).astype(jnp.bfloat16)
+    rows = jnp.dot(compact, slots, preferred_element_type=jnp.float32).astype(jnp.float16)
     rows = lax.all_gather(rows, "local", axis=0, tiled=True)
 
-    gate = jnp.where(owner == 0, rows[:, width], rows[:, width + 1]).astype(jnp.float32)
-    back, gate_part = expert_backward(
-        rows[:, :width], gate, saved_gate, saved_up, w_gate[0], w_up[0], w_down[0]
+    upward = lax.dot_general(
+        rows[:, :width].astype(jnp.bfloat16),
+        w_down[0],
+        (((1,), (1,)), ((), ())),
+        preferred_element_type=jnp.float32,
     )
-    column = lax.broadcasted_iota(jnp.int32, (back.shape[0], EXTRA), 1)
-    extra = jnp.where(column == owner, gate_part[:, None], 0.0).astype(jnp.bfloat16)
-    parts = jnp.concatenate([back, extra], axis=1)
+    extra = rows[:, width:].astype(jnp.float32)
+    parts = hidden_parts(
+        owner, upward, extra, saved_gate, saved_up, w_gate[0], w_up[0]
+    )
     sums = lax.psum_scatter(parts, "local", scatter_dimension=0, tiled=True)
 
     home = exchange(

time: 256 us -> 232 us (0.906)
  waiting for transfers between devices: 147 us -> 84.1 us
  blocking collectives: 72.2 us -> 95.5 us
  starting transfers between devices: 0.08 us -> 18.3 us
  matrix products: 10.1 us -> 4.69 us
  Pallas kernels: 0 us -> 2.81 us
  local copies, waits for them, and re-layouts: 5.81 us -> 8.61 us
    all_gather x1 -> x0, waiting for transfers between devices: 69.2 us -> none  [on_device(): rows = lax.all_gather(rows, 'local', axis=0, tiled=True)]
    all_gather x0 -> x1, blocking collectives: none -> 58.4 us  [on_device(): rows = lax.all_gather(rows, 'local', axis=0, tiled=True)]
    all_to_all x2 -> x1, blocking collectives: 72.2 us -> 37.1 us  [exchange(): lax.all_to_all(x.reshape(count, 1, width), 'node', split_axis=0, concat_a...]
    all_to_all x0 -> x1, starting transfers between devices: none -> 18.2 us  [exchange(): lax.all_to_all(x.reshape(count, 1, width), 'node', split_axis=0, concat_a...]
    all_to_all x0 -> x1, waiting for transfers between devices: none -> 17.1 us  [exchange(): lax.all_to_all(x.reshape(count, 1, width), 'node', split_axis=0, concat_a...]
    reduce_scatter x1, waiting for transfers between devices: 77.6 us -> 67 us  [on_device(): sums = lax.psum_scatter(parts, 'local', scatter_dimension=0, tiled=True)]
    dot_general x4 -> x3, matrix products: 7.13 us -> 2.41 us  [the longest x1 1.17 us: on_device(): send_rows = jnp.dot(pick, scaled, preferred_element_type=jnp.float32)]
    pallas_call x0 -> x1, Pallas kernels: none -> 2.81 us  [hidden_parts(): pl.pallas_call(hidden_kernel, grid=(rows // block,), in_specs=[pl.BlockSp...]
where the time goes in v2:
time: 232 us
  blocking collectives  95.5 us (41%)
  waiting for transfers between devices  84.1 us (36%)
  starting transfers between devices  18.3 us (8%)
  between operations  14.3 us (6%)
  local copies, waits for them, and re-layouts  8.61 us (4%)
  matrix products  4.69 us (2%)
  other arithmetic  3.48 us (2%)
  Pallas kernels  2.81 us (1%)
    reduce_scatter x1, waiting for transfers between devices, on_device(): sums = lax.psum_scatter(parts, 'local', scatter_dimension=0, tiled=True)  67 us
    all_gather x1, blocking collectives, on_device(): rows = lax.all_gather(rows, 'local', axis=0, tiled=True)  58.4 us
    all_to_all x1, blocking collectives, exchange(): lax.all_to_all(x.reshape(count, 1, width), 'node', split_axis=0, concat_a...  37.1 us
    all_to_all x1, starting transfers between devices, exchange(): lax.all_to_all(x.reshape(count, 1, width), 'node', split_axis=0, concat_a...  18.2 us
    all_to_all x1, waiting for transfers between devices, exchange(): lax.all_to_all(x.reshape(count, 1, width), 'node', split_axis=0, concat_a...  17.1 us
    unnamed x22, local copies, waits for them, and re-layouts  7.73 us
  transfers between devices with their start and end apart: 2, of which 2 were waited for; matrix products, arithmetic and copies ran while one was open for 0% of the time, Pallas kernels for 0%

profile of v2, /device:TPU:1, one launch (start us, length us, event | category | flops | bytes accessed | tf_op | source)
XLA Modules:
  0.0 231.7 jit_solution(5034739832146383534)
XLA Ops:
  7.2 0.0 copy-start
  7.2 0.8 copy.55
  8.0 0.9 fusion.6
  9.0 0.1 iota_compare_fusion.1
  9.1 0.1 fusion.3
  9.2 0.8 copy.72
  10.0 0.1 select_reduce_fusion.1
  10.1 0.1 copy.60
  10.2 0.1 copy.61
  10.3 1.2 convolution_convert_fusion
  11.5 0.1 concatenate.3
  11.6 0.5 broadcast.403
  12.2 0.9 reduce.4
  13.1 1.1 reshape.213
  14.2 18.2 %all-to-all-start = ((bf16[64,2,1856]{2,1,0:T(2,128)(2,1)}), bf16[64,2,1856]{2,1,0:T(2,128)(2,1)S(1)}, u32[]{:S(2)}, u32[]{:S(2)}) async-start(bf16[64,2,1856]{2,1,0:T(2,128)(2,1)} %reshape.213), calls=%async_computation | async-start | bytes 983040 | tf_op jit(solution)/shard_map/all_to_all | solution.py:83
  32.5 0.0 reduce-scatter.2.cloned.1.call-start
  32.5 17.1 %all-to-all-done = bf16[64,2,1856]{2,1,0:T(2,128)(2,1)S(1)} async-done(((bf16[64,2,1856]{2,1,0:T(2,128)(2,1)}), bf16[64,2,1856]{2,1,0:T(2,128)(2,1)S(1)}, u32[]{:S(2)}, u32[]{:S(2)}) %all-to-all-start) | async-done | bytes 475168 | tf_op jit(solution)/shard_map/all_to_all | solution.py:83
  49.6 0.8 reshape.214
  50.4 0.1 copy.76
  50.5 0.1 compare_reduce_fusion
  50.6 0.1 reduce-window.8
  50.7 0.1 subtract_reduce_fusion
  50.8 0.2 convolution_convert_fusion.2
  51.0 58.4 %all-gather.1 = f16[512,3712]{1,0:T(8,128)(2,1)S(1)} all-gather(f16[32,3712]{1,0:T(8,128)(2,1)S(1)} %convolution_convert_fusion.2), channel_id=1, replica_groups=mesh['node'=64,'local'=16] {'local'}, dimensions={0}, use_global_device_ids=true | all-gather | bytes 4038656 | tf_op jit(solution)/shard_map/all_gather | solution.py:129
  109.5 0.0 copy-start.2
  109.5 0.0 copy-start.3
  109.5 0.0 copy-start.4
  109.5 0.0 copy-start.5
  109.5 1.1 fusion.1.up_ref
  110.6 0.0 copy-done.2
  110.7 0.3 copy-done.3
  111.0 0.0 copy-done.4
  111.0 0.0 copy-done.5
  111.0 2.8 %shard_map.95 = bf16[512,3712]{1,0:T(8,128)(2,1)S(1)} custom-call(s32[1]{0:T(128)} %bitcast.7.owner_ref, f32[512,128]{1,0:T(8,128)S(1)} %fusion.1.up_ref, f32[512,128]{1,0:T(8,128)S(1)} %slice_convert_fusion.2.extra_ref, bf16[512,128]{1,0:T(8,128)(2,1)S(1)} %copy-done.4, bf16[512,128]{1,0:T(8,128)(2,1)S(1)} %copy-done.5, bf16[3584,128]{1,0:T(8,128)(2,1)S(1)} %bitcast.38, ...), custom_call_target="tpu_custom_call" | custom-call | flops 939524096 | bytes 5505024 | tf_op jit(solution)/shard_map/pallas_call | solution.py:46
  113.8 0.0 copy-start.1
  113.8 1.8 copy-done.1
  115.6 0.0 reduce-scatter.2.cloned.1.call-update
  115.7 67.0 %reduce-scatter.2.cloned.1.call-done = bf16[32,3712]{1,0:T(8,128)(2,1)} async-done(((bf16[512,3712]{1,0:T(8,128)(2,1)}), bf16[32,3712]{1,0:T(8,128)(2,1)}) %reduce-scatter.2.cloned.1.call-update) | async-done | bytes 237584 | tf_op jit(solution)/shard_map/reduce_scatter | solution.py:141
  182.6 1.3 fusion
  183.9 0.9 reduce.5
  184.9 0.4 reshape.215
  185.2 37.1 %all_to_all.10 = bf16[64,2,1856]{2,1,0:T(2,128)(2,1)S(1)} all-to-all(bf16[64,2,1856]{2,1,0:T(2,128)(2,1)S(1)} %reshape.215), channel_id=1, replica_groups=mesh['node'=64,'local'=16] {'node'}, dimensions={0} | all-to-all | bytes 950272 | tf_op jit(solution)/shard_map/all_to_all | solution.py:83
  222.3 0.8 reshape.216
  223.1 0.1 copy.75
  223.2 0.8 convolution_convert_fusion.3
  224.0 0.1 copy.70
  224.1 0.1 select_reduce_fusion
  224.2 0.7 copy.67
  (16 shorter events, 0.1 us)
Async XLA Ops:
  7.2 102.3 %copy-start = (bf16[1,128,3584]{2,1,0:T(8,128)(2,1)S(1)}, bf16[1,128,3584]{2,1,0:T(8,128)(2,1)}, u32[]{:S(2)}) copy-start(bf16[1,128,3584]{2,1,0:T(8,128)(2,1)} %param.15) | copy-start | bytes 2752516
  14.2 35.4 %all-to-all-start = ((bf16[64,2,1856]{2,1,0:T(2,128)(2,1)}), bf16[64,2,1856]{2,1,0:T(2,128)(2,1)S(1)}, u32[]{:S(2)}, u32[]{:S(2)}) async-start(bf16[64,2,1856]{2,1,0:T(2,128)(2,1)} %reshape.213), calls=%async_computation | async-start | bytes 983040 | tf_op jit(solution)/shard_map/all_to_all | solution.py:83
  32.5 150.2 %reduce-scatter.2.cloned.1.call-start = ((), (), s32[]{:S(2)}) async-start(), calls=%async_computation.3 | async-start | bytes 4038656 | tf_op jit(solution)/shard_map/reduce_scatter | solution.py:141
  109.5 1.2 copy-start.2
  109.5 1.4 copy-start.3
  109.5 1.4 copy-start.4
  109.5 1.5 copy-start.5
  113.8 1.8 copy-start.1
Sparse Core Ops, SparseCore 0:
  115.8 66.8 reduce-scatter.1

commit v3 on v2

--- a/solution.py
+++ b/solution.py
@@ -11,8 +11,10 @@
 EXTRA = 128
 
 
-def hidden_kernel(owner_ref, up_ref, extra_ref, sgate_ref, sup_ref, wg_ref, wu_ref, out_ref):
-    owner = owner_ref[0]
+def hidden_kernel(where_ref, up_ref, extra_ref, sgate_ref, sup_ref, mine_ref, others_ref):
+    owner, parity = where_ref[0], where_ref[1]
+    rows, hidden = up_ref.shape
+    group = mine_ref.shape[1]
     extra = extra_ref[...]
     column = lax.broadcasted_iota(jnp.int32, extra.shape, 1)
     gate = jnp.sum(jnp.where(column == owner, extra, 0.0), axis=1, keepdims=True)
@@ -26,44 +28,123 @@
     scaled = gate * upward
     grad_gate = (scaled * pre_up * sigma * (1.0 + pre_gate * (1.0 - sigma))).astype(jnp.bfloat16)
     grad_up = (scaled * active).astype(jnp.bfloat16)
-    dims = (((1,), (1,)), ((), ()))
-    width = wg_ref.shape[0]
-    step = width // 7 if width % 896 == 0 else width
-    for start in range(0, width, step):
-        cols = slice(start, start + step)
-        back = lax.dot_general(grad_gate, wg_ref[cols, :], dims, preferred_element_type=jnp.float32)
-        back += lax.dot_general(grad_up, wu_ref[cols, :], dims, preferred_element_type=jnp.float32)
-        out_ref[:, cols] = back.astype(jnp.bfloat16)
-    out_ref[:, width:] = jnp.where(column == owner, gate_part, 0.0).astype(jnp.bfloat16)
-
-
-def hidden_parts(owner, upward, extra, saved_gate, saved_up, w_gate, w_up):
+    terms = jnp.where(column == owner, gate_part, 0.0).astype(jnp.bfloat16)
+    for index in range(rows // group):
+        here = slice(index * group, (index + 1) * group)
+        for keep, ref in ((parity, mine_ref), (1 - parity, others_ref)):
+
+            @pl.when(keep == index % 2)
+            def _(ref=ref, here=here, index=index):
+                ref[index // 2, :, :hidden] = grad_gate[here]
+                ref[index // 2, :, hidden : 2 * hidden] = grad_up[here]
+                ref[index // 2, :, 2 * hidden :] = terms[here]
+
+
+def hidden_grads(where, upward, extra, saved_gate, saved_up, group):
     rows, hidden = upward.shape
-    width = w_gate.shape[0]
-    block = 128 if rows % 128 == 0 else rows
-    by_rows = lambda cols: pl.BlockSpec((block, cols), lambda i: (i, 0))
-    whole = lambda shape: pl.BlockSpec(shape, lambda i: (0, 0))
+    out = jax.ShapeDtypeStruct((rows // group // 2, group, 2 * hidden + EXTRA), jnp.bfloat16)
     return pl.pallas_call(
         hidden_kernel,
-        grid=(rows // block,),
+        in_specs=[pl.BlockSpec(memory_space=pltpu.SMEM)]
+        + [pl.BlockSpec(memory_space=pltpu.VMEM)] * 4,
+        out_specs=[pl.BlockSpec(memory_space=pltpu.VMEM)] * 2,
+        out_shape=[out, out],
+        compiler_params=pltpu.CompilerParams(vmem_limit_bytes=8 * 2**20),
+        cost_estimate=pl.CostEstimate(
+            flops=20 * rows * hidden, bytes_accessed=8 * rows * hidden, transcendentals=rows * hidden
+        ),
+    )(where, upward, extra, saved_gate, saved_up)
+
+
+def parts_kernel(mine_ref, low_h_ref, high_h_ref, own_ref, low_ref, high_ref, out_ref):
+    step = pl.program_id(0)
+    steps = pl.num_programs(0)
+    cols, depth = own_ref.shape
+    dims = (((1,), (1,)), ((), ()))
+
+    def times(x, w):
+        return lax.dot_general(x, w, dims, preferred_element_type=jnp.float32)
+
+    def write(other_h_ref, other_ref):
+        back = times(mine_ref[:, :depth], own_ref[...])
+        back += times(other_h_ref[:, :depth], other_ref[...])
+        out_ref[:, pl.ds(pl.multiple_of(step * cols, 128), cols)] = back.astype(jnp.bfloat16)
+
+    @pl.when(step < steps // 2)
+    def _():
+        write(low_h_ref, low_ref)
+
+    @pl.when(step >= steps // 2)
+    def _():
+        write(high_h_ref, high_ref)
+
+    @pl.when(step == 0)
+    def _():
+        out_ref[:, out_ref.shape[1] - EXTRA :] = mine_ref[:, depth:] + high_h_ref[:, depth:]
+
+
+def device_parts(mine, low_h, high_h, own, low, high):
+    rows = mine.shape[0]
+    width, depth = own.shape
+    steps = 4
+    cols = width // steps
+    whole = lambda x: pl.BlockSpec(x.shape, lambda i: (0, 0))
+    return pl.pallas_call(
+        parts_kernel,
+        grid=(steps,),
         in_specs=[
-            pl.BlockSpec(memory_space=pltpu.SMEM),
-            by_rows(hidden),
-            by_rows(EXTRA),
-            by_rows(hidden),
-            by_rows(hidden),
-            whole((width, hidden)),
-            whole((width, hidden)),
+            whole(mine),
+            whole(low_h),
+            whole(high_h),
+            pl.BlockSpec((cols, depth), lambda i: (i, 0)),
+            pl.BlockSpec((cols, depth), lambda i: (jnp.minimum(i, steps // 2 - 1), 0)),
+            pl.BlockSpec((cols, depth), lambda i: (jnp.maximum(i - steps // 2, 0), 0)),
         ],
-        out_specs=by_rows(width + EXTRA),
+        out_specs=pl.BlockSpec((rows, width + EXTRA), lambda i: (0, 0)),
         out_shape=jax.ShapeDtypeStruct((rows, width + EXTRA), jnp.bfloat16),
         compiler_params=pltpu.CompilerParams(vmem_limit_bytes=24 * 2**20),
         cost_estimate=pl.CostEstimate(
-            flops=4 * rows * width * hidden,
-            bytes_accessed=4 * width * hidden + 2 * rows * width,
-            transcendentals=rows * hidden,
+            flops=4 * rows * width * depth,
+            bytes_accessed=4 * width * depth + 2 * rows * width,
+            transcendentals=0,
         ),
-    )(owner.reshape(1), upward, extra, saved_gate, saved_up, w_gate, w_up)
+    )(mine, low_h, high_h, own, low, high)
+
+
+def ring_sum(parts, count, stride, place):
+    size = count * stride
+    right = [(i, (i + stride) % size) for i in range(size)]
+    left = [(i, (i - stride) % size) for i in range(size)]
+    rows = parts.shape[0] // count
+    cut = (parts.shape[1] // 256) * 128
+
+    def block(offset):
+        start = lax.rem(place + offset + count, count) * rows
+        return lax.dynamic_slice_in_dim(parts, start, rows)
+
+    def add(x, y):
+        return (x.astype(jnp.float32) + y.astype(jnp.float32)).astype(jnp.bfloat16)
+
+    half = count // 2
+    far = block(half)
+    one = lax.ppermute(far[:, :cut], "local", right)
+    two = lax.ppermute(far[:, cut:], "local", left)
+    for offset in range(half - 1, 0, -1):
+        here, there = block(offset), block(-offset)
+        one, two = lax.optimization_barrier((one, two))
+        if offset == half - 1:
+            one = jnp.concatenate([add(here[:, :cut], one), here[:, cut:]], axis=1)
+            two = jnp.concatenate([there[:, :cut], add(there[:, cut:], two)], axis=1)
+        else:
+            one, two = add(here, one), add(there, two)
+        one = lax.ppermute(one, "local", right)
+        two = lax.ppermute(two, "local", left)
+    own = block(0).astype(jnp.float32)
+    if half == 1:
+        both = jnp.concatenate([one, two], axis=1).astype(jnp.float32)
+    else:
+        both = one.astype(jnp.float32) + two.astype(jnp.float32)
+    return (own + both).astype(jnp.bfloat16)
 
 
 def power_scale(rows):
@@ -79,11 +160,7 @@
 
 
 def exchange(x):
-    count, width = x.shape
-    x = lax.all_to_all(
-        x.reshape(count, 1, width), "node", split_axis=0, concat_axis=0, tiled=True
-    )
-    return x.reshape(count, width)
+    return lax.all_to_all(x, "node", split_axis=0, concat_axis=0, tiled=True)
 
 
 def on_device(
@@ -94,7 +171,6 @@
     tok_count, width = output_gradient.shape
     live_count = tok_count * NODES_TOK
     shard_count = local_count // EXP_NODE
-    owner = lax.axis_index("local") // shard_count
 
     pairs = expert_ids.reshape(tok_count, NODES_TOK, EXP_NODE)
     dest_node = pairs[:, :, 0] // EXP_NODE
@@ -113,11 +189,21 @@
             send_rows.astype(jnp.bfloat16),
             send_gate.astype(jnp.bfloat16),
             send_shift.astype(jnp.bfloat16),
-            jnp.zeros((node_count, EXTRA - EXP_NODE - 1), jnp.bfloat16),
+            jnp.zeros((node_count, 2 * EXTRA - EXP_NODE - 1), jnp.bfloat16),
         ],
         axis=1,
-    )
-    slots = exchange(send)
+    ).reshape(node_count, 2, -1)
+
+    place = lax.axis_index("local")
+    parity = lax.rem(place, 2)
+    half = width // 2
+    low_pairs = [(i, i ^ 1) for i in range(local_count)]
+    high_pairs = [(i, (i + 2 * (i % 2) - 1) % local_count) for i in range(local_count)]
+    own = jnp.concatenate([w_gate[0], w_up[0]], axis=1)
+    send, own = lax.optimization_barrier((send, own))
+    slots = exchange(send).reshape(node_count, -1)
+    low = lax.ppermute(own[:half], "local", low_pairs)
+    high = lax.ppermute(own[half:], "local", high_pairs)
 
     live = (slots[:, width] > 0).astype(jnp.int32)
     rank = jnp.cumsum(live) - live
@@ -125,7 +211,8 @@
         live[None] > 0
     )
     compact = compact.astype(jnp.bfloat16)
-    rows = jnp.dot(compact, slots, preferred_element_type=jnp.float32).astype(jnp.float16)
+    rows = jnp.dot(compact, slots, preferred_element_type=jnp.float32)
+    rows = rows[:, : width + EXTRA].astype(jnp.float16)
     rows = lax.all_gather(rows, "local", axis=0, tiled=True)
 
     upward = lax.dot_general(
@@ -134,17 +221,25 @@
         (((1,), (1,)), ((), ())),
         preferred_element_type=jnp.float32,
     )
-    extra = rows[:, width:].astype(jnp.float32)
-    parts = hidden_parts(
-        owner, upward, extra, saved_gate, saved_up, w_gate[0], w_up[0]
-    )
-    sums = lax.psum_scatter(parts, "local", scatter_dimension=0, tiled=True)
-
-    home = exchange(
-        lax.dot_general(
-            compact, sums, (((0,), (0,)), ((), ())), preferred_element_type=jnp.float32
-        ).astype(jnp.bfloat16)
-    )
+    mine, others = hidden_grads(
+        jnp.stack([place // shard_count, parity]),
+        upward,
+        rows[:, width:].astype(jnp.float32),
+        saved_gate,
+        saved_up,
+        live_count,
+    )
+    low_h = lax.ppermute(others, "local", low_pairs)
+    high_h = lax.ppermute(others, "local", high_pairs)
+    flat = lambda x: x.reshape(-1, x.shape[-1])
+    parts = device_parts(flat(mine), flat(low_h), flat(high_h), own, low, high)
+    sums = ring_sum(parts, local_count // 2, 2, place // 2)
+
+    back = lax.dot_general(
+        compact, sums, (((0,), (0,)), ((), ())), preferred_element_type=jnp.float32
+    ).astype(jnp.bfloat16)
+    back = jnp.pad(back, ((0, 0), (0, EXTRA))).reshape(node_count, 2, -1)
+    home = exchange(back).reshape(node_count, -1)
     grad_in = lax.dot_general(
         pick, home[:, :width], (((0,), (0,)), ((), ())), preferred_element_type=jnp.float32
     ).astype(jnp.bfloat16)

time: 232 us -> 227 us (0.978); the launches traced: 232 us -> 224 us
  waiting for transfers between devices: 84.1 us -> 36.4 us
  starting transfers between devices: 18.3 us -> 65 us
  between operations: 14.3 us -> 1.16 us
  blocking collectives: 95.5 us -> 99.2 us
  other arithmetic: 3.48 us -> 5.84 us
    reduce_scatter x1 -> x0, waiting for transfers between devices: 67 us -> none  [on_device(): sums = lax.psum_scatter(parts, 'local', scatter_dimension=0, tiled=True)]
    ppermute x0 -> x12, starting transfers between devices: none -> 46.8 us  [the longest x1 11.6 us: on_device(): high = lax.ppermute(own[half:], 'local', high_pairs)]
    ppermute x0 -> x12, waiting for transfers between devices: none -> 34.3 us  [the longest x3 20.2 us: ring_sum(): one = lax.ppermute(one, 'local', right)]
    all_to_all x1, waiting for transfers between devices: 17.1 us -> 2.16 us  [exchange(): return lax.all_to_all(x, 'node', split_axis=0, concat_axis=0, tiled=True)]
    all_gather x1, blocking collectives: 58.4 us -> 62.5 us  [on_device(): rows = lax.all_gather(rows, 'local', axis=0, tiled=True)]
    unnamed x22 -> x20, local copies, waits for them, and re-layouts: 7.73 us -> 4.3 us
    convert_element_type x1 -> x5, other arithmetic: 0.02 us -> 2.44 us  [the longest x4 2.43 us: add(): return (x.astype(jnp.float32) + y.astype(jnp.float32)).astype(jnp.bfloat16)]
    pallas_call x1 -> x2, Pallas kernels: 2.81 us -> 4.7 us  [the longest x1 3.68 us: device_parts(): pl.pallas_call(parts_kernel, grid=(steps,), in_specs=[whole(mine), whole(...]
  transfers between devices with their start and end apart: 2 -> 13, of which waited for: 2 -> 9; matrix products, arithmetic and copies ran while one was open for 0% -> 2% of each run, Pallas kernels for 0% -> 0%
where the time goes in v3:
time: 227 us; the launch traced here: 224 us
  blocking collectives  99.2 us (44%)
  starting transfers between devices  65 us (29%)
  waiting for transfers between devices  36.4 us (16%)
  local copies, waits for them, and re-layouts  7.19 us (3%)
  other arithmetic  5.84 us (3%)
  Pallas kernels  4.7 us (2%)
  matrix products  4.69 us (2%)
    all_gather x1, blocking collectives, on_device(): rows = lax.all_gather(rows, 'local', axis=0, tiled=True)  62.5 us
    all_to_all x1, blocking collectives, exchange(): return lax.all_to_all(x, 'node', split_axis=0, concat_axis=0, tiled=True)  36.7 us
    ppermute x3, waiting for transfers between devices, ring_sum(): one = lax.ppermute(one, 'local', right)  20.2 us
    all_to_all x1, starting transfers between devices, exchange(): return lax.all_to_all(x, 'node', split_axis=0, concat_axis=0, tiled=True)  18.2 us
    ppermute x1, starting transfers between devices, on_device(): high = lax.ppermute(own[half:], 'local', high_pairs)  11.6 us
    ppermute x3, starting transfers between devices, ring_sum(): two = lax.ppermute(two, 'local', left)  11.2 us
    ppermute x3, starting transfers between devices, ring_sum(): one = lax.ppermute(one, 'local', right)  9.76 us
    ppermute x1, waiting for transfers between devices, on_device(): high_h = lax.ppermute(others, 'local', high_pairs)  4.58 us
  transfers between devices with their start and end apart: 13, of which 9 were waited for; matrix products, arithmetic and copies ran while one was open for 2% of the time, Pallas kernels for 0%

profile of v3, /device:TPU:1, one launch (start us, length us, event | category | flops | bytes accessed | tf_op | source)
XLA Modules:
  0.0 224.2 jit_solution(16975720856993510719)
XLA Ops:
  0.6 0.8 copy.24
  1.6 0.9 fusion.6
  2.6 0.1 fusion.2
  2.7 1.2 convolution_convert_fusion
  3.9 0.8 copy.38
  4.8 0.1 copy.29
  4.9 0.1 copy.30
  5.1 0.9 reshape.209
  6.0 1.7 pad_maximum_fusion.own_ref
  7.7 18.2 %all-to-all-start = ((bf16[64,2,1920]{2,1,0:T(2,128)(2,1)}), bf16[64,2,1920]{2,1,0:T(2,128)(2,1)S(1)}, u32[]{:S(2)}, u32[]{:S(2)}) async-start(bf16[64,2,1920]{2,1,0:T(2,128)(2,1)} %reshape.209), calls=%async_computation | async-start | bytes 983040 | tf_op jit(solution)/shard_map/all_to_all | solution.py:163
  25.9 1.4 fusion.55
  27.3 1.9 collective-permute-start.2
  29.2 11.6 %collective-permute-start.3 = (bf16[1792,256]{1,0:T(8,128)(2,1)}, bf16[1792,256]{1,0:T(8,128)(2,1)}, u32[]{:S(2)}, u32[]{:S(2)}) collective-permute-start(bf16[1792,256]{1,0:T(8,128)(2,1)} %get-tuple-element.36), channel_id=1, source_target_pairs={{0,15},{1,2},{2,1},{3,4},{4,3},{5,6},{6,5},{7,8},{8,7},{9,10},{10,... | collective-permute-start | bytes 2752520 | tf_op jit(solution)/shard_map/ppermute | solution.py:206
  40.9 2.2 all-to-all-done
  43.1 0.8 copy-done.4
  43.9 1.1 copy.36
  45.0 0.1 compare_reduce_fusion
  45.2 0.1 subtract_reduce_fusion
  45.3 0.2 fusion.12
  45.5 62.5 %all-gather.1 = f16[512,3712]{1,0:T(8,128)(2,1)S(1)} all-gather(f16[32,3712]{1,0:T(8,128)(2,1)S(1)} %slice_convert_fusion.2), channel_id=1, replica_groups=mesh['node'=64,'local'=16] {'local'}, dimensions={0}, use_global_device_ids=true | all-gather | bytes 4038656 | tf_op jit(solution)/shard_map/all_gather | solution.py:216
  108.1 1.1 fusion.up_ref
  109.2 1.0 shard_map.95
  110.2 4.1 %collective-permute-start = (bf16[8,32,384]{2,1,0:T(8,128)(2,1)S(1)}, bf16[8,32,384]{2,1,0:T(8,128)(2,1)S(1)}, u32[]{:S(2)}, u32[]{:S(2)}) collective-permute-start(bf16[8,32,384]{2,1,0:T(8,128)(2,1)S(1)} %get-tuple-element.14), channel_id=1, source_target_pairs={{0,1},{1,0},{2,3},{3,2},{4,5},{5,4},{6,7},{7,6},{8,9},{9,8},{10,11... | collective-permute-start | bytes 589832 | tf_op jit(solution)/shard_map/ppermute | solution.py:232
  114.3 2.0 collective-permute-start.1
  116.5 0.9 collective-permute-done
  117.4 4.6 %collective-permute-done.1 = bf16[8,32,384]{2,1,0:T(8,128)(2,1)S(1)} collective-permute-done((bf16[8,32,384]{2,1,0:T(8,128)(2,1)S(1)}, bf16[8,32,384]{2,1,0:T(8,128)(2,1)S(1)}, u32[]{:S(2)}, u32[]{:S(2)}) %collective-permute-start.1) | collective-permute-done | bytes 196640 | tf_op jit(solution)/shard_map/ppermute | solution.py:233
  122.0 3.7 %shard_map.96 = bf16[256,3712]{1,0:T(8,128)(2,1)S(1)} custom-call(bf16[256,384]{1,0:T(8,128)(2,1)S(1)} %bitcast.35, bf16[256,384]{1,0:T(8,128)(2,1)S(1)} %bitcast.36, bf16[256,384]{1,0:T(8,128)(2,1)S(1)} %bitcast.37, bf16[3584,256]{1,0:T(8,128)(2,1)S(1)} %pad_maximum_fusion.own_ref, bf16[1792,256]{1,0:T(8,128)(2,1)} %collective-permute-done.2.low_ref, ...), custom_call_target="tpu_custom_call" | custom-call | flops 939524096 | bytes 5505024 | tf_op jit(solution)/shard_map/pallas_call | solution.py:92
  125.7 1.9 collective-permute-start.5
  127.7 4.3 %collective-permute-start.4 = (bf16[32,1792]{1,0:T(8,128)(2,1)S(1)}, bf16[32,1792]{1,0:T(8,128)(2,1)S(1)}, u32[]{:S(2)}, u32[]{:S(2)}) collective-permute-start(bf16[32,1792]{1,0:T(8,128)(2,1)S(1)} %get-tuple-element.33), channel_id=1, source_target_pairs={{0,2},{1,3},{2,4},{3,5},{4,6},{5,7},{6,8},{7,9},{8,10},{9,11},{10,... | collective-permute-start | bytes 344072 | tf_op jit(solution)/shard_map/ppermute | solution.py:130
  131.9 4.3 %collective-permute-done.4 = bf16[32,1792]{1,0:T(8,128)(2,1)S(1)} collective-permute-done((bf16[32,1792]{1,0:T(8,128)(2,1)S(1)}, bf16[32,1792]{1,0:T(8,128)(2,1)S(1)}, u32[]{:S(2)}, u32[]{:S(2)}) %collective-permute-start.4) | collective-permute-done | bytes 114720 | tf_op jit(solution)/shard_map/ppermute | solution.py:130
  136.3 2.1 collective-permute-start.7
  138.5 4.1 %collective-permute-start.6 = (bf16[32,3712]{1,0:T(8,128)(2,1)S(1)}, bf16[32,3712]{1,0:T(8,128)(2,1)S(1)}, u32[]{:S(2)}, u32[]{:S(2)}) collective-permute-start(bf16[32,3712]{1,0:T(8,128)(2,1)S(1)} %pad_maximum_fusion.1), channel_id=1, source_target_pairs={{0,2},{1,3},{2,4},{3,5},{4,6},{5,7},{6,8},{7,9},{8,10},{9,11},{10,... | collective-permute-start | bytes 712712 | tf_op jit(solution)/shard_map/ppermute | solution.py:140
  142.6 2.4 %collective-permute-done.7 = bf16[32,3712]{1,0:T(8,128)(2,1)S(1)} collective-permute-done((bf16[32,3712]{1,0:T(8,128)(2,1)S(1)}, bf16[32,3712]{1,0:T(8,128)(2,1)S(1)}, u32[]{:S(2)}, u32[]{:S(2)}) %collective-permute-start.7) | collective-permute-done | bytes 237600 | tf_op jit(solution)/shard_map/ppermute | solution.py:141
  145.1 2.8 %collective-permute-done.6 = bf16[32,3712]{1,0:T(8,128)(2,1)S(1)} collective-permute-done((bf16[32,3712]{1,0:T(8,128)(2,1)S(1)}, bf16[32,3712]{1,0:T(8,128)(2,1)S(1)}, u32[]{:S(2)}, u32[]{:S(2)}) %collective-permute-start.6) | collective-permute-done | bytes 237600 | tf_op jit(solution)/shard_map/ppermute | solution.py:140
  147.9 1.2 add_convert_fusion.3
  149.0 3.3 %collective-permute-start.8 = (bf16[32,3712]{1,0:T(8,128)(2,1)S(1)}, bf16[32,3712]{1,0:T(8,128)(2,1)S(1)}, u32[]{:S(2)}, u32[]{:S(2)}) collective-permute-start(bf16[32,3712]{1,0:T(8,128)(2,1)S(1)} %get-tuple-element.31), channel_id=1, source_target_pairs={{0,2},{1,3},{2,4},{3,5},{4,6},{5,7},{6,8},{7,9},{8,10},{9,11},{10,... | collective-permute-start | bytes 712712 | tf_op jit(solution)/shard_map/ppermute | solution.py:140
  152.4 4.1 %collective-permute-start.9 = (bf16[32,3712]{1,0:T(8,128)(2,1)S(1)}, bf16[32,3712]{1,0:T(8,128)(2,1)S(1)}, u32[]{:S(2)}, u32[]{:S(2)}) collective-permute-start(bf16[32,3712]{1,0:T(8,128)(2,1)S(1)} %get-tuple-element.30), channel_id=1, source_target_pairs={{0,14},{1,15},{2,0},{3,1},{4,2},{5,3},{6,4},{7,5},{8,6},{9,7},{10,... | collective-permute-start | bytes 712712 | tf_op jit(solution)/shard_map/ppermute | solution.py:141
  156.5 8.8 %collective-permute-done.8 = bf16[32,3712]{1,0:T(8,128)(2,1)S(1)} collective-permute-done((bf16[32,3712]{1,0:T(8,128)(2,1)S(1)}, bf16[32,3712]{1,0:T(8,128)(2,1)S(1)}, u32[]{:S(2)}, u32[]{:S(2)}) %collective-permute-start.8) | collective-permute-done | bytes 237600 | tf_op jit(solution)/shard_map/ppermute | solution.py:140
  165.3 1.2 add_convert_fusion.2
  166.5 2.4 %collective-permute-start.10 = (bf16[32,3712]{1,0:T(8,128)(2,1)S(1)}, bf16[32,3712]{1,0:T(8,128)(2,1)S(1)}, u32[]{:S(2)}, u32[]{:S(2)}) collective-permute-start(bf16[32,3712]{1,0:T(8,128)(2,1)S(1)} %get-tuple-element.28), channel_id=1, source_target_pairs={{0,2},{1,3},{2,4},{3,5},{4,6},{5,7},{6,8},{7,9},{8,10},{9,11},{10,... | collective-permute-start | bytes 712712 | tf_op jit(solution)/shard_map/ppermute | solution.py:140
  168.9 5.0 %collective-permute-start.11 = (bf16[32,3712]{1,0:T(8,128)(2,1)S(1)}, bf16[32,3712]{1,0:T(8,128)(2,1)S(1)}, u32[]{:S(2)}, u32[]{:S(2)}) collective-permute-start(bf16[32,3712]{1,0:T(8,128)(2,1)S(1)} %get-tuple-element.29), channel_id=1, source_target_pairs={{0,14},{1,15},{2,0},{3,1},{4,2},{5,3},{6,4},{7,5},{8,6},{9,7},{10,... | collective-permute-start | bytes 712712 | tf_op jit(solution)/shard_map/ppermute | solution.py:141
  173.9 8.6 %collective-permute-done.10 = bf16[32,3712]{1,0:T(8,128)(2,1)S(1)} collective-permute-done((bf16[32,3712]{1,0:T(8,128)(2,1)S(1)}, bf16[32,3712]{1,0:T(8,128)(2,1)S(1)}, u32[]{:S(2)}, u32[]{:S(2)}) %collective-permute-start.10) | collective-permute-done | bytes 237600 | tf_op jit(solution)/shard_map/ppermute | solution.py:140
  182.5 1.8 collective-permute-done.11
  184.3 1.3 convolution_convert_fusion.1
  185.6 0.1 reshape.214
  185.8 36.7 %all_to_all.10 = bf16[64,2,1920]{2,1,0:T(2,128)(2,1)S(1)} all-to-all(bf16[64,2,1920]{2,1,0:T(2,128)(2,1)S(1)} %reshape.214), channel_id=1, replica_groups=mesh['node'=64,'local'=16] {'node'}, dimensions={0} | all-to-all | bytes 983040 | tf_op jit(solution)/shard_map/all_to_all | solution.py:163
  222.5 0.8 convolution_convert_fusion.2
  223.6 0.7 copy.34
  (48 shorter events, 1.1 us)
Async XLA Ops:
  0.6 107.4 %copy-start = (bf16[1,128,3584]{2,1,0:T(8,128)(2,1)S(1)}, bf16[1,128,3584]{2,1,0:T(8,128)(2,1)}, u32[]{:S(2)}) copy-start(bf16[1,128,3584]{2,1,0:T(8,128)(2,1)} %param.15) | copy-start | bytes 2752516
  7.7 35.4 %all-to-all-start = ((bf16[64,2,1920]{2,1,0:T(2,128)(2,1)}), bf16[64,2,1920]{2,1,0:T(2,128)(2,1)S(1)}, u32[]{:S(2)}, u32[]{:S(2)}) async-start(bf16[64,2,1920]{2,1,0:T(2,128)(2,1)} %reshape.209), calls=%async_computation | async-start | bytes 983040 | tf_op jit(solution)/shard_map/all_to_all | solution.py:163
  27.3 89.2 %collective-permute-start.2 = (bf16[1792,256]{1,0:T(8,128)(2,1)}, bf16[1792,256]{1,0:T(8,128)(2,1)}, u32[]{:S(2)}, u32[]{:S(2)}) collective-permute-start(bf16[1792,256]{1,0:T(8,128)(2,1)} %get-tuple-element.37), channel_id=1, source_target_pairs={{0,1},{1,0},{2,3},{3,2},{4,5},{5,4},{6,7},{7,6},{8,9},{9,8},{10,11... | collective-permute-start | bytes 2752520 | tf_op jit(solution)/shard_map/ppermute | solution.py:205
  29.2 87.2 %collective-permute-start.3 = (bf16[1792,256]{1,0:T(8,128)(2,1)}, bf16[1792,256]{1,0:T(8,128)(2,1)}, u32[]{:S(2)}, u32[]{:S(2)}) collective-permute-start(bf16[1792,256]{1,0:T(8,128)(2,1)} %get-tuple-element.36), channel_id=1, source_target_pairs={{0,15},{1,2},{2,1},{3,4},{4,3},{5,6},{6,5},{7,8},{8,7},{9,10},{10,... | collective-permute-start | bytes 2752520 | tf_op jit(solution)/shard_map/ppermute | solution.py:206
  43.1 0.8 copy-start.4
  45.3 62.7 %copy-start.5 = (s32[64]{0:T(128)}, s32[64]{0:T(128)S(1)}, u32[]{:S(2)}) copy-start(s32[64]{0:T(128)S(1)} %subtract_reduce_fusion) | copy-start | bytes 772
  108.0 1.1 copy-start.2
  108.1 1.1 copy-start.3
  110.2 7.2 %collective-permute-start = (bf16[8,32,384]{2,1,0:T(8,128)(2,1)S(1)}, bf16[8,32,384]{2,1,0:T(8,128)(2,1)S(1)}, u32[]{:S(2)}, u32[]{:S(2)}) collective-permute-start(bf16[8,32,384]{2,1,0:T(8,128)(2,1)S(1)} %get-tuple-element.14), channel_id=1, source_target_pairs={{0,1},{1,0},{2,3},{3,2},{4,5},{5,4},{6,7},{7,6},{8,9},{9,8},{10,11... | collective-permute-start | bytes 589832 | tf_op jit(solution)/shard_map/ppermute | solution.py:232
  114.3 7.6 %collective-permute-start.1 = (bf16[8,32,384]{2,1,0:T(8,128)(2,1)S(1)}, bf16[8,32,384]{2,1,0:T(8,128)(2,1)S(1)}, u32[]{:S(2)}, u32[]{:S(2)}) collective-permute-start(bf16[8,32,384]{2,1,0:T(8,128)(2,1)S(1)} %get-tuple-element.14), channel_id=1, source_target_pairs={{0,15},{1,2},{2,1},{3,4},{4,3},{5,6},{6,5},{7,8},{8,7},{9,10},{10,... | collective-permute-start | bytes 589832 | tf_op jit(solution)/shard_map/ppermute | solution.py:233
  125.7 12.8 %copy-start.1 = (bf16[256,3712]{1,0:T(8,128)(2,1)}, bf16[256,3712]{1,0:T(8,128)(2,1)S(1)}, u32[]{:S(2)}) copy-start(bf16[256,3712]{1,0:T(8,128)(2,1)S(1)} %shard_map.96) | copy-start | bytes 5701636
  125.7 10.6 %collective-permute-start.5 = (bf16[32,1920]{1,0:T(8,128)(2,1)S(1)}, bf16[32,1920]{1,0:T(8,128)(2,1)S(1)}, u32[]{:S(2)}, u32[]{:S(2)}) collective-permute-start(bf16[32,1920]{1,0:T(8,128)(2,1)S(1)} %get-tuple-element.34), channel_id=1, source_target_pairs={{0,14},{1,15},{2,0},{3,1},{4,2},{5,3},{6,4},{7,5},{8,6},{9,7},{10,... | collective-permute-start | bytes 368648 | tf_op jit(solution)/shard_map/ppermute | solution.py:131
  127.7 8.6 %collective-permute-start.4 = (bf16[32,1792]{1,0:T(8,128)(2,1)S(1)}, bf16[32,1792]{1,0:T(8,128)(2,1)S(1)}, u32[]{:S(2)}, u32[]{:S(2)}) collective-permute-start(bf16[32,1792]{1,0:T(8,128)(2,1)S(1)} %get-tuple-element.33), channel_id=1, source_target_pairs={{0,2},{1,3},{2,4},{3,5},{4,6},{5,7},{6,8},{7,9},{8,10},{9,11},{10,... | collective-permute-start | bytes 344072 | tf_op jit(solution)/shard_map/ppermute | solution.py:130
  136.3 48.0 %copy-start.6 = (s32[64]{0:T(128)S(1)}, s32[64]{0:T(128)}, u32[]{:S(2)}) copy-start(s32[64]{0:T(128)} %copy-done.5) | copy-start | bytes 772
  136.3 8.7 %collective-permute-start.7 = (bf16[32,3712]{1,0:T(8,128)(2,1)S(1)}, bf16[32,3712]{1,0:T(8,128)(2,1)S(1)}, u32[]{:S(2)}, u32[]{:S(2)}) collective-permute-start(bf16[32,3712]{1,0:T(8,128)(2,1)S(1)} %pad_maximum_fusion.2), channel_id=1, source_target_pairs={{0,14},{1,15},{2,0},{3,1},{4,2},{5,3},{6,4},{7,5},{8,6},{9,7},{10,... | collective-permute-start | bytes 712712 | tf_op jit(solution)/shard_map/ppermute | solution.py:141
  138.5 9.3 %collective-permute-start.6 = (bf16[32,3712]{1,0:T(8,128)(2,1)S(1)}, bf16[32,3712]{1,0:T(8,128)(2,1)S(1)}, u32[]{:S(2)}, u32[]{:S(2)}) collective-permute-start(bf16[32,3712]{1,0:T(8,128)(2,1)S(1)} %pad_maximum_fusion.1), channel_id=1, source_target_pairs={{0,2},{1,3},{2,4},{3,5},{4,6},{5,7},{6,8},{7,9},{8,10},{9,11},{10,... | collective-permute-start | bytes 712712 | tf_op jit(solution)/shard_map/ppermute | solution.py:140
  149.0 16.3 %collective-permute-start.8 = (bf16[32,3712]{1,0:T(8,128)(2,1)S(1)}, bf16[32,3712]{1,0:T(8,128)(2,1)S(1)}, u32[]{:S(2)}, u32[]{:S(2)}) collective-permute-start(bf16[32,3712]{1,0:T(8,128)(2,1)S(1)} %get-tuple-element.31), channel_id=1, source_target_pairs={{0,2},{1,3},{2,4},{3,5},{4,6},{5,7},{6,8},{7,9},{8,10},{9,11},{10,... | collective-permute-start | bytes 712712 | tf_op jit(solution)/shard_map/ppermute | solution.py:140
  152.4 12.9 %collective-permute-start.9 = (bf16[32,3712]{1,0:T(8,128)(2,1)S(1)}, bf16[32,3712]{1,0:T(8,128)(2,1)S(1)}, u32[]{:S(2)}, u32[]{:S(2)}) collective-permute-start(bf16[32,3712]{1,0:T(8,128)(2,1)S(1)} %get-tuple-element.30), channel_id=1, source_target_pairs={{0,14},{1,15},{2,0},{3,1},{4,2},{5,3},{6,4},{7,5},{8,6},{9,7},{10,... | collective-permute-start | bytes 712712 | tf_op jit(solution)/shard_map/ppermute | solution.py:141
  166.5 16.0 %collective-permute-start.10 = (bf16[32,3712]{1,0:T(8,128)(2,1)S(1)}, bf16[32,3712]{1,0:T(8,128)(2,1)S(1)}, u32[]{:S(2)}, u32[]{:S(2)}) collective-permute-start(bf16[32,3712]{1,0:T(8,128)(2,1)S(1)} %get-tuple-element.28), channel_id=1, source_target_pairs={{0,2},{1,3},{2,4},{3,5},{4,6},{5,7},{6,8},{7,9},{8,10},{9,11},{10,... | collective-permute-start | bytes 712712 | tf_op jit(solution)/shard_map/ppermute | solution.py:140
  168.9 15.4 %collective-permute-start.11 = (bf16[32,3712]{1,0:T(8,128)(2,1)S(1)}, bf16[32,3712]{1,0:T(8,128)(2,1)S(1)}, u32[]{:S(2)}, u32[]{:S(2)}) collective-permute-start(bf16[32,3712]{1,0:T(8,128)(2,1)S(1)} %get-tuple-element.29), channel_id=1, source_target_pairs={{0,14},{1,15},{2,0},{3,1},{4,2},{5,3},{6,4},{7,5},{8,6},{9,7},{10,... | collective-permute-start | bytes 712712 | tf_op jit(solution)/shard_map/ppermute | solution.py:141

commit v4 on v3

--- a/solution.py
+++ b/solution.py
@@ -11,104 +11,108 @@
 EXTRA = 128
 
 
-def hidden_kernel(where_ref, up_ref, extra_ref, sgate_ref, sup_ref, mine_ref, others_ref):
-    owner, parity = where_ref[0], where_ref[1]
-    rows, hidden = up_ref.shape
-    group = mine_ref.shape[1]
-    extra = extra_ref[...]
-    column = lax.broadcasted_iota(jnp.int32, extra.shape, 1)
-    gate = jnp.sum(jnp.where(column == owner, extra, 0.0), axis=1, keepdims=True)
-    shift = jnp.sum(jnp.where(column == EXP_NODE, extra, 0.0), axis=1, keepdims=True)
-    upward = up_ref[...] * jnp.exp2(-shift)
-    pre_gate = sgate_ref[...].astype(jnp.float32)
-    pre_up = sup_ref[...].astype(jnp.float32)
-    sigma = jax.nn.sigmoid(pre_gate)
-    active = pre_gate * sigma
-    gate_part = jnp.sum(active * pre_up * upward, axis=1, keepdims=True)
-    scaled = gate * upward
-    grad_gate = (scaled * pre_up * sigma * (1.0 + pre_gate * (1.0 - sigma))).astype(jnp.bfloat16)
-    grad_up = (scaled * active).astype(jnp.bfloat16)
-    terms = jnp.where(column == owner, gate_part, 0.0).astype(jnp.bfloat16)
-    for index in range(rows // group):
-        here = slice(index * group, (index + 1) * group)
-        for keep, ref in ((parity, mine_ref), (1 - parity, others_ref)):
-
-            @pl.when(keep == index % 2)
-            def _(ref=ref, here=here, index=index):
-                ref[index // 2, :, :hidden] = grad_gate[here]
-                ref[index // 2, :, hidden : 2 * hidden] = grad_up[here]
-                ref[index // 2, :, 2 * hidden :] = terms[here]
-
-
-def hidden_grads(where, upward, extra, saved_gate, saved_up, group):
-    rows, hidden = upward.shape
-    out = jax.ShapeDtypeStruct((rows // group // 2, group, 2 * hidden + EXTRA), jnp.bfloat16)
-    return pl.pallas_call(
-        hidden_kernel,
-        in_specs=[pl.BlockSpec(memory_space=pltpu.SMEM)]
-        + [pl.BlockSpec(memory_space=pltpu.VMEM)] * 4,
-        out_specs=[pl.BlockSpec(memory_space=pltpu.VMEM)] * 2,
-        out_shape=[out, out],
-        compiler_params=pltpu.CompilerParams(vmem_limit_bytes=8 * 2**20),
-        cost_estimate=pl.CostEstimate(
-            flops=20 * rows * hidden, bytes_accessed=8 * rows * hidden, transcendentals=rows * hidden
-        ),
-    )(where, upward, extra, saved_gate, saved_up)
-
-
-def parts_kernel(mine_ref, low_h_ref, high_h_ref, own_ref, low_ref, high_ref, out_ref):
+def parts_kernel(
+    owner_ref,
+    extra_ref,
+    rows_ref,
+    down_own_ref,
+    down_low_ref,
+    down_high_ref,
+    saved_own_ref,
+    saved_low_ref,
+    saved_high_ref,
+    own_gate_ref,
+    own_up_ref,
+    low_ref,
+    high_ref,
+    out_ref,
+    grads_ref,
+):
     step = pl.program_id(0)
-    steps = pl.num_programs(0)
-    cols, depth = own_ref.shape
+    steps = pl.num_programs(0) - 1
+    cols, hidden = own_gate_ref.shape
     dims = (((1,), (1,)), ((), ()))
 
     def times(x, w):
         return lax.dot_general(x, w, dims, preferred_element_type=jnp.float32)
 
-    def write(other_h_ref, other_ref):
-        back = times(mine_ref[:, :depth], own_ref[...])
-        back += times(other_h_ref[:, :depth], other_ref[...])
-        out_ref[:, pl.ds(pl.multiple_of(step * cols, 128), cols)] = back.astype(jnp.bfloat16)
-
-    @pl.when(step < steps // 2)
-    def _():
-        write(low_h_ref, low_ref)
-
-    @pl.when(step >= steps // 2)
-    def _():
-        write(high_h_ref, high_ref)
-
     @pl.when(step == 0)
     def _():
-        out_ref[:, out_ref.shape[1] - EXTRA :] = mine_ref[:, depth:] + high_h_ref[:, depth:]
-
-
-def device_parts(mine, low_h, high_h, own, low, high):
-    rows = mine.shape[0]
-    width, depth = own.shape
+        extra = extra_ref[...]
+        column = lax.broadcasted_iota(jnp.int32, extra.shape, 1)
+
+        def pick_column(index):
+            return jnp.sum(jnp.where(column == index, extra, 0.0), axis=1, keepdims=True)
+
+        undo = jnp.exp2(-pick_column(EXP_NODE))
+        rows = rows_ref[...]
+        shards = (
+            (down_own_ref, saved_own_ref),
+            (down_low_ref, saved_low_ref),
+            (down_high_ref, saved_high_ref),
+        )
+        terms = jnp.zeros(extra.shape, jnp.float32)
+        for index, (down_ref, saved_ref) in enumerate(shards):
+            owner = owner_ref[index]
+            upward = times(rows, down_ref[...]) * undo
+            pre_gate = saved_ref[:, :hidden].astype(jnp.float32)
+            pre_up = saved_ref[:, hidden:].astype(jnp.float32)
+            sigma = jax.nn.sigmoid(pre_gate)
+            active = pre_gate * sigma
+            scaled = pick_column(owner) * upward
+            grad_gate = scaled * pre_up * sigma * (1.0 + pre_gate * (1.0 - sigma))
+            grads_ref[index, :, :hidden] = grad_gate.astype(jnp.bfloat16)
+            grads_ref[index, :, hidden:] = (scaled * active).astype(jnp.bfloat16)
+            if index != 1:
+                gate_part = jnp.sum(active * pre_up * upward, axis=1, keepdims=True)
+                terms += jnp.where(column == owner, gate_part, 0.0)
+        out_ref[:, out_ref.shape[1] - EXTRA :] = terms.astype(jnp.bfloat16)
+
+    def write(index, other_ref):
+        back = times(grads_ref[index], other_ref[...])
+        back += times(grads_ref[0, :, :hidden], own_gate_ref[...])
+        back += times(grads_ref[0, :, hidden:], own_up_ref[...])
+        start = pl.multiple_of((step - 1) * cols, 128)
+        out_ref[:, pl.ds(start, cols)] = back.astype(jnp.bfloat16)
+
+    @pl.when((step > 0) & (step <= steps // 2))
+    def _():
+        write(1, low_ref)
+
+    @pl.when(step > steps // 2)
+    def _():
+        write(2, high_ref)
+
+
+def device_parts(owners, extra, rows, downs, saved_own, w_gate, w_up, low, high):
+    count, depth = saved_own.shape
+    width, hidden = w_gate.shape
     steps = 4
-    cols = width // steps
+    half, cols = width // 2, width // steps
     whole = lambda x: pl.BlockSpec(x.shape, lambda i: (0, 0))
+    tail = pl.BlockSpec((count, depth), lambda i: (half // count, 0))
     return pl.pallas_call(
         parts_kernel,
-        grid=(steps,),
-        in_specs=[
-            whole(mine),
-            whole(low_h),
-            whole(high_h),
-            pl.BlockSpec((cols, depth), lambda i: (i, 0)),
-            pl.BlockSpec((cols, depth), lambda i: (jnp.minimum(i, steps // 2 - 1), 0)),
-            pl.BlockSpec((cols, depth), lambda i: (jnp.maximum(i - steps // 2, 0), 0)),
+        grid=(steps + 1,),
+        in_specs=[pl.BlockSpec(memory_space=pltpu.SMEM), whole(extra), whole(rows)]
+        + [whole(x) for x in downs]
+        + [whole(saved_own), tail, tail]
+        + [
+            pl.BlockSpec((cols, hidden), lambda i: (jnp.maximum(i - 1, 0), 0)),
+            pl.BlockSpec((cols, hidden), lambda i: (jnp.maximum(i - 1, 0), 0)),
+            pl.BlockSpec((cols, depth), lambda i: (jnp.clip(i - 1, 0, steps // 2 - 1), 0)),
+            pl.BlockSpec((cols, depth), lambda i: (jnp.maximum(i - 1 - steps // 2, 0), 0)),
         ],
-        out_specs=pl.BlockSpec((rows, width + EXTRA), lambda i: (0, 0)),
-        out_shape=jax.ShapeDtypeStruct((rows, width + EXTRA), jnp.bfloat16),
-        compiler_params=pltpu.CompilerParams(vmem_limit_bytes=24 * 2**20),
+        out_specs=pl.BlockSpec((count, width + EXTRA), lambda i: (0, 0)),
+        out_shape=jax.ShapeDtypeStruct((count, width + EXTRA), jnp.bfloat16),
+        scratch_shapes=[pltpu.VMEM((3, count, depth), jnp.bfloat16)],
+        compiler_params=pltpu.CompilerParams(vmem_limit_bytes=32 * 2**20),
         cost_estimate=pl.CostEstimate(
-            flops=4 * rows * width * depth,
-            bytes_accessed=4 * width * depth + 2 * rows * width,
-            transcendentals=0,
+            flops=14 * count * width * hidden,
+            bytes_accessed=14 * width * hidden + 4 * count * width,
+            transcendentals=3 * count * hidden,
         ),
-    )(mine, low_h, high_h, own, low, high)
+    )(owners, extra, rows, *downs, saved_own, low, high, w_gate, w_up, low, high)
 
 
 def ring_sum(parts, count, stride, place):
@@ -199,11 +203,23 @@
     half = width // 2
     low_pairs = [(i, i ^ 1) for i in range(local_count)]
     high_pairs = [(i, (i + 2 * (i % 2) - 1) % local_count) for i in range(local_count)]
+    down = w_down[0]
+    down_low = lax.ppermute(down, "local", low_pairs)
+    down_high = lax.ppermute(down, "local", high_pairs)
+    saved = jnp.concatenate([saved_gate, saved_up], axis=1)
+    saved = saved.reshape(local_count // 2, 2, live_count, -1)
+    mine, others = (
+        lax.dynamic_index_in_dim(saved, which, axis=1, keepdims=False).reshape(
+            local_count // 2 * live_count, -1
+        )
+        for which in (parity, 1 - parity)
+    )
     own = jnp.concatenate([w_gate[0], w_up[0]], axis=1)
-    send, own = lax.optimization_barrier((send, own))
+    low, high = jnp.concatenate([own[:half], others]), jnp.concatenate([own[half:], others])
+    send, low, high = lax.optimization_barrier((send, low, high))
     slots = exchange(send).reshape(node_count, -1)
-    low = lax.ppermute(own[:half], "local", low_pairs)
-    high = lax.ppermute(own[half:], "local", high_pairs)
+    low = lax.ppermute(low, "local", low_pairs)
+    high = lax.ppermute(high, "local", high_pairs)
 
     live = (slots[:, width] > 0).astype(jnp.int32)
     rank = jnp.cumsum(live) - live
@@ -213,26 +229,27 @@
     compact = compact.astype(jnp.bfloat16)
     rows = jnp.dot(compact, slots, preferred_element_type=jnp.float32)
     rows = rows[:, : width + EXTRA].astype(jnp.float16)
-    rows = lax.all_gather(rows, "local", axis=0, tiled=True)
-
-    upward = lax.dot_general(
+    rows = lax.all_gather(
+        rows,
+        "local",
+        axis=0,
+        tiled=True,
+        axis_index_groups=[list(range(i, local_count, 2)) for i in range(2)],
+    )
+
+    step = 2 * parity - 1
+    shards = jnp.stack([place, place - step, lax.rem(place + step + local_count, local_count)])
+    parts = device_parts(
+        shards // shard_count,
+        rows[:, width:].astype(jnp.float32),
         rows[:, :width].astype(jnp.bfloat16),
-        w_down[0],
-        (((1,), (1,)), ((), ())),
-        preferred_element_type=jnp.float32,
-    )
-    mine, others = hidden_grads(
-        jnp.stack([place // shard_count, parity]),
-        upward,
-        rows[:, width:].astype(jnp.float32),
-        saved_gate,
-        saved_up,
-        live_count,
-    )
-    low_h = lax.ppermute(others, "local", low_pairs)
-    high_h = lax.ppermute(others, "local", high_pairs)
-    flat = lambda x: x.reshape(-1, x.shape[-1])
-    parts = device_parts(flat(mine), flat(low_h), flat(high_h), own, low, high)
+        [down, down_low, down_high],
+        mine,
+        w_gate[0],
+        w_up[0],
+        low,
+        high,
+    )
     sums = ring_sum(parts, local_count // 2, 2, place // 2)
 
     back = lax.dot_general(

time: 227 us -> 221 us (0.974)
  waiting for transfers between devices: 36.4 us -> 24.2 us
  blocking collectives: 99.2 us -> 106 us
    ppermute x3, waiting for transfers between devices: 20.2 us -> 12.2 us  [ring_sum(): one = lax.ppermute(one, 'local', right)]
    all_gather x1, blocking collectives: 62.5 us -> 68.9 us  [on_device(): lax.all_gather(rows, 'local', axis=0, tiled=True, axis_index_groups=[list...]
    ppermute x4, waiting for transfers between devices: 5.52 us -> 0.01 us  [the longest x1 0.01 us: on_device(): down_high = lax.ppermute(down, 'local', high_pairs)]
    ppermute x1, starting transfers between devices: 1.92 us -> 4.75 us  [ring_sum(): two = lax.ppermute(far[:, cut:], 'local', left)]
    ppermute x1, starting transfers between devices: 4.26 us -> 1.92 us  [ring_sum(): one = lax.ppermute(far[:, :cut], 'local', right)]
    pallas_call x2 -> x1, Pallas kernels: 4.7 us -> 6.54 us  [device_parts(): pl.pallas_call(parts_kernel, grid=(steps + 1,), in_specs=[pl.BlockSpec(me...]
  transfers between devices with their start and end apart: 13 -> 13, of which waited for: 9 -> 6; matrix products, arithmetic and copies ran while one was open for 2% -> 2% of each run, Pallas kernels for 0% -> 0%
where the time goes in v4:
time: 221 us; the launch traced here: 220 us
  blocking collectives  106 us (48%)
  starting transfers between devices  64.4 us (29%)
  waiting for transfers between devices  24.2 us (11%)
  other arithmetic  7.92 us (4%)
  Pallas kernels  6.54 us (3%)
  local copies, waits for them, and re-layouts  5.87 us (3%)
  matrix products  4.24 us (2%)
    all_gather x1, blocking collectives, on_device(): lax.all_gather(rows, 'local', axis=0, tiled=True, axis_index_groups=[list...  68.9 us
    all_to_all x1, blocking collectives, exchange(): return lax.all_to_all(x, 'node', split_axis=0, concat_axis=0, tiled=True)  36.7 us
    all_to_all x1, starting transfers between devices, exchange(): return lax.all_to_all(x, 'node', split_axis=0, concat_axis=0, tiled=True)  18.2 us
    ppermute x3, waiting for transfers between devices, ring_sum(): one = lax.ppermute(one, 'local', right)  12.2 us
    ppermute x1, starting transfers between devices, on_device(): down_high = lax.ppermute(down, 'local', high_pairs)  11.6 us
    ppermute x3, starting transfers between devices, ring_sum(): one = lax.ppermute(one, 'local', right)  11.4 us
    ppermute x3, starting transfers between devices, ring_sum(): two = lax.ppermute(two, 'local', left)  9.6 us
    pallas_call x1, Pallas kernels, device_parts(): pl.pallas_call(parts_kernel, grid=(steps + 1,), in_specs=[pl.BlockSpec(me...  6.54 us
  transfers between devices with their start and end apart: 13, of which 6 were waited for; matrix products, arithmetic and copies ran while one was open for 2% of the time, Pallas kernels for 0%

profile of v4, /device:TPU:1, one launch (start us, length us, event | category | flops | bytes accessed | tf_op | source)
XLA Modules:
  0.0 219.9 jit_solution(12163053163835476043)
XLA Ops:
  0.7 0.9 copy.28
  1.7 0.9 fusion.5
  2.7 0.1 fusion.1
  2.8 1.2 convolution_convert_fusion
  4.0 0.8 copy.46
  4.8 0.1 select_reduce_fusion.1
  4.8 0.1 copy.33
  5.0 0.1 copy.34
  5.1 0.1 concatenate.21
  5.2 0.9 reshape.211
  6.2 0.1 fusion.2
  6.3 1.5 pad_maximum_fusion
  7.8 18.2 %all-to-all-start = ((bf16[64,2,1920]{2,1,0:T(2,128)(2,1)}), bf16[64,2,1920]{2,1,0:T(2,128)(2,1)S(1)}, u32[]{:S(2)}, u32[]{:S(2)}) async-start(bf16[64,2,1920]{2,1,0:T(2,128)(2,1)} %reshape.211), calls=%async_computation | async-start | bytes 983040 | tf_op jit(solution)/shard_map/all_to_all | solution.py:167
  26.0 1.9 collective-permute-start
  28.0 11.6 %collective-permute-start.1 = (bf16[128,3584]{1,0:T(8,128)(2,1)}, bf16[128,3584]{1,0:T(8,128)(2,1)}, u32[]{:S(2)}, u32[]{:S(2)}) collective-permute-start(bf16[128,3584]{1,0:T(8,128)(2,1)} %bitcast.13.down_own_ref), channel_id=1, source_target_pairs={{0,15},{1,2},{2,1},{3,4},{4,3},{5,6},{6,5},{7,8},{8,7},{9,10},{10,... | collective-permute-start | bytes 2752520 | tf_op jit(solution)/shard_map/ppermute | solution.py:208
  39.6 1.9 collective-permute-start.2
  41.5 3.1 %collective-permute-start.3 = (bf16[2048,256]{1,0:T(8,128)(2,1)}, bf16[2048,256]{1,0:T(8,128)(2,1)}, u32[]{:S(2)}, u32[]{:S(2)}) collective-permute-start(bf16[2048,256]{1,0:T(8,128)(2,1)} %get-tuple-element.13), channel_id=1, source_target_pairs={{0,15},{1,2},{2,1},{3,4},{4,3},{5,6},{6,5},{7,8},{8,7},{9,10},{10,... | collective-permute-start | bytes 3145736 | tf_op jit(solution)/shard_map/ppermute | solution.py:222
  44.8 0.8 copy-done.3
  45.6 1.1 copy.44
  46.7 0.6 compare_reduce_fusion
  47.3 0.7 reduce-window.8
  48.0 0.9 subtract_reduce_fusion
  48.8 0.9 fusion.11
  49.8 68.9 %all-gather.1 = f16[256,3712]{1,0:T(8,128)(2,1)S(1)} all-gather(f16[32,3712]{1,0:T(8,128)(2,1)S(1)} %slice_convert_fusion.1), channel_id=1, replica_groups={{0,2,4,6,8,10,12,14},{1,3,5,7,9,11,13,15},{16,18,20,22,24,26,28,30},{17..., dimensions={0}, use_global_device_ids=true | all-gather | bytes 2138112 | tf_op jit(solution)/shard_map/all_gather | solution.py:232
  118.6 0.2 slice_convert_fusion.rows_ref
  118.9 6.5 %shard_map.95 = bf16[256,3712]{1,0:T(8,128)(2,1)S(1)} custom-call(s32[3]{0:T(128)S(1)} %and_select_fusion.1.owner_ref, f32[256,128]{1,0:T(8,128)S(1)} %slice_convert_fusion.2.extra_ref, bf16[256,3584]{1,0:T(8,128)(2,1)S(1)} %slice_convert_fusion.rows_ref, bf16[128,3584]{1,0:T(8,128)(2,1)} %bitcast.13.down_own_ref, ...), custom_call_target="tpu_custom_call" | custom-call | flops 1644167168 | bytes 10092544 | tf_op jit(solution)/shard_map/pallas_call | solution.py:94
  125.5 4.7 %collective-permute-start.5 = (bf16[32,1920]{1,0:T(8,128)(2,1)S(1)}, bf16[32,1920]{1,0:T(8,128)(2,1)S(1)}, u32[]{:S(2)}, u32[]{:S(2)}) collective-permute-start(bf16[32,1920]{1,0:T(8,128)(2,1)S(1)} %get-tuple-element.32), channel_id=1, source_target_pairs={{0,14},{1,15},{2,0},{3,1},{4,2},{5,3},{6,4},{7,5},{8,6},{9,7},{10,... | collective-permute-start | bytes 368648 | tf_op jit(solution)/shard_map/ppermute | solution.py:135
  130.3 1.9 collective-permute-start.4
  132.2 5.7 %collective-permute-done.4 = bf16[32,1792]{1,0:T(8,128)(2,1)S(1)} collective-permute-done((bf16[32,1792]{1,0:T(8,128)(2,1)S(1)}, bf16[32,1792]{1,0:T(8,128)(2,1)S(1)}, u32[]{:S(2)}, u32[]{:S(2)}) %collective-permute-start.4) | collective-permute-done | bytes 114720 | tf_op jit(solution)/shard_map/ppermute | solution.py:134
  138.0 1.9 collective-permute-start.7
  140.0 4.2 %collective-permute-start.6 = (bf16[32,3712]{1,0:T(8,128)(2,1)S(1)}, bf16[32,3712]{1,0:T(8,128)(2,1)S(1)}, u32[]{:S(2)}, u32[]{:S(2)}) collective-permute-start(bf16[32,3712]{1,0:T(8,128)(2,1)S(1)} %pad_maximum_fusion.4), channel_id=1, source_target_pairs={{0,2},{1,3},{2,4},{3,5},{4,6},{5,7},{6,8},{7,9},{8,10},{9,11},{10,... | collective-permute-start | bytes 712712 | tf_op jit(solution)/shard_map/ppermute | solution.py:144
  144.3 1.4 collective-permute-done.7
  145.8 3.5 %collective-permute-done.6 = bf16[32,3712]{1,0:T(8,128)(2,1)S(1)} collective-permute-done((bf16[32,3712]{1,0:T(8,128)(2,1)S(1)}, bf16[32,3712]{1,0:T(8,128)(2,1)S(1)}, u32[]{:S(2)}, u32[]{:S(2)}) %collective-permute-start.6) | collective-permute-done | bytes 237600 | tf_op jit(solution)/shard_map/ppermute | solution.py:144
  149.2 1.2 add_convert_fusion.3
  150.4 3.1 %collective-permute-start.8 = (bf16[32,3712]{1,0:T(8,128)(2,1)S(1)}, bf16[32,3712]{1,0:T(8,128)(2,1)S(1)}, u32[]{:S(2)}, u32[]{:S(2)}) collective-permute-start(bf16[32,3712]{1,0:T(8,128)(2,1)S(1)} %get-tuple-element.29), channel_id=1, source_target_pairs={{0,2},{1,3},{2,4},{3,5},{4,6},{5,7},{6,8},{7,9},{8,10},{9,11},{10,... | collective-permute-start | bytes 712712 | tf_op jit(solution)/shard_map/ppermute | solution.py:144
  153.5 4.2 %collective-permute-start.9 = (bf16[32,3712]{1,0:T(8,128)(2,1)S(1)}, bf16[32,3712]{1,0:T(8,128)(2,1)S(1)}, u32[]{:S(2)}, u32[]{:S(2)}) collective-permute-start(bf16[32,3712]{1,0:T(8,128)(2,1)S(1)} %get-tuple-element.28), channel_id=1, source_target_pairs={{0,14},{1,15},{2,0},{3,1},{4,2},{5,3},{6,4},{7,5},{8,6},{9,7},{10,... | collective-permute-start | bytes 712712 | tf_op jit(solution)/shard_map/ppermute | solution.py:145
  157.8 5.0 %collective-permute-done.8 = bf16[32,3712]{1,0:T(8,128)(2,1)S(1)} collective-permute-done((bf16[32,3712]{1,0:T(8,128)(2,1)S(1)}, bf16[32,3712]{1,0:T(8,128)(2,1)S(1)}, u32[]{:S(2)}, u32[]{:S(2)}) %collective-permute-start.8) | collective-permute-done | bytes 237600 | tf_op jit(solution)/shard_map/ppermute | solution.py:144
  162.8 1.2 add_convert_fusion.2
  164.0 4.0 %collective-permute-start.10 = (bf16[32,3712]{1,0:T(8,128)(2,1)S(1)}, bf16[32,3712]{1,0:T(8,128)(2,1)S(1)}, u32[]{:S(2)}, u32[]{:S(2)}) collective-permute-start(bf16[32,3712]{1,0:T(8,128)(2,1)S(1)} %get-tuple-element.26), channel_id=1, source_target_pairs={{0,2},{1,3},{2,4},{3,5},{4,6},{5,7},{6,8},{7,9},{8,10},{9,11},{10,... | collective-permute-start | bytes 712712 | tf_op jit(solution)/shard_map/ppermute | solution.py:144
  168.0 3.4 %collective-permute-start.11 = (bf16[32,3712]{1,0:T(8,128)(2,1)S(1)}, bf16[32,3712]{1,0:T(8,128)(2,1)S(1)}, u32[]{:S(2)}, u32[]{:S(2)}) collective-permute-start(bf16[32,3712]{1,0:T(8,128)(2,1)S(1)} %get-tuple-element.27), channel_id=1, source_target_pairs={{0,14},{1,15},{2,0},{3,1},{4,2},{5,3},{6,4},{7,5},{8,6},{9,7},{10,... | collective-permute-start | bytes 712712 | tf_op jit(solution)/shard_map/ppermute | solution.py:145
  171.4 3.8 %collective-permute-done.10 = bf16[32,3712]{1,0:T(8,128)(2,1)S(1)} collective-permute-done((bf16[32,3712]{1,0:T(8,128)(2,1)S(1)}, bf16[32,3712]{1,0:T(8,128)(2,1)S(1)}, u32[]{:S(2)}, u32[]{:S(2)}) %collective-permute-start.10) | collective-permute-done | bytes 237600 | tf_op jit(solution)/shard_map/ppermute | solution.py:144
  175.2 4.8 %collective-permute-done.11 = bf16[32,3712]{1,0:T(8,128)(2,1)S(1)} collective-permute-done((bf16[32,3712]{1,0:T(8,128)(2,1)S(1)}, bf16[32,3712]{1,0:T(8,128)(2,1)S(1)}, u32[]{:S(2)}, u32[]{:S(2)}) %collective-permute-start.11) | collective-permute-done | bytes 237600 | tf_op jit(solution)/shard_map/ppermute | solution.py:145
  180.0 1.3 convolution_convert_fusion.1
  181.4 0.1 reshape.216
  181.5 36.7 %all_to_all.10 = bf16[64,2,1920]{2,1,0:T(2,128)(2,1)S(1)} all-to-all(bf16[64,2,1920]{2,1,0:T(2,128)(2,1)S(1)} %reshape.216), channel_id=1, replica_groups=mesh['node'=64,'local'=16] {'node'}, dimensions={0} | all-to-all | bytes 983040 | tf_op jit(solution)/shard_map/all_to_all | solution.py:167
  218.2 0.8 convolution_convert_fusion.2
  219.1 0.1 select_reduce_fusion
  219.3 0.7 copy.40
  (49 shorter events, 0.8 us)
Async XLA Ops:
  0.6 5.5 %copy-start.5 = (bf16[512,128]{1,0:T(8,128)(2,1)S(1)}, bf16[512,128]{1,0:T(8,128)(2,1)}, u32[]{:S(2)}) copy-start(bf16[512,128]{1,0:T(8,128)(2,1)} %param.11) | copy-start | bytes 393220
  0.6 5.5 %copy-start.4 = (bf16[512,128]{1,0:T(8,128)(2,1)S(1)}, bf16[512,128]{1,0:T(8,128)(2,1)}, u32[]{:S(2)}) copy-start(bf16[512,128]{1,0:T(8,128)(2,1)} %param.12) | copy-start | bytes 393220
  0.7 5.5 %copy-start.1 = (bf16[1,3584,128]{2,1,0:T(8,128)(2,1)S(1)}, bf16[1,3584,128]{2,1,0:T(8,128)(2,1)}, u32[]{:S(2)}) copy-start(bf16[1,3584,128]{2,1,0:T(8,128)(2,1)} %param.13) | copy-start | bytes 2752516
  0.7 5.5 %copy-start = (bf16[1,3584,128]{2,1,0:T(8,128)(2,1)S(1)}, bf16[1,3584,128]{2,1,0:T(8,128)(2,1)}, u32[]{:S(2)}) copy-start(bf16[1,3584,128]{2,1,0:T(8,128)(2,1)} %param.14) | copy-start | bytes 2752516
  7.8 37.0 %all-to-all-start = ((bf16[64,2,1920]{2,1,0:T(2,128)(2,1)}), bf16[64,2,1920]{2,1,0:T(2,128)(2,1)S(1)}, u32[]{:S(2)}, u32[]{:S(2)}) async-start(bf16[64,2,1920]{2,1,0:T(2,128)(2,1)} %reshape.211), calls=%async_computation | async-start | bytes 983040 | tf_op jit(solution)/shard_map/all_to_all | solution.py:167
  26.0 92.8 %collective-permute-start = (bf16[128,3584]{1,0:T(8,128)(2,1)}, bf16[128,3584]{1,0:T(8,128)(2,1)}, u32[]{:S(2)}, u32[]{:S(2)}) collective-permute-start(bf16[128,3584]{1,0:T(8,128)(2,1)} %bitcast.13.down_own_ref), channel_id=1, source_target_pairs={{0,1},{1,0},{2,3},{3,2},{4,5},{5,4},{6,7},{7,6},{8,9},{9,8},{10,11... | collective-permute-start | bytes 2752520 | tf_op jit(solution)/shard_map/ppermute | solution.py:207
  28.0 90.9 %collective-permute-start.1 = (bf16[128,3584]{1,0:T(8,128)(2,1)}, bf16[128,3584]{1,0:T(8,128)(2,1)}, u32[]{:S(2)}, u32[]{:S(2)}) collective-permute-start(bf16[128,3584]{1,0:T(8,128)(2,1)} %bitcast.13.down_own_ref), channel_id=1, source_target_pairs={{0,15},{1,2},{2,1},{3,4},{4,3},{5,6},{6,5},{7,8},{8,7},{9,10},{10,... | collective-permute-start | bytes 2752520 | tf_op jit(solution)/shard_map/ppermute | solution.py:208
  39.6 79.3 %collective-permute-start.2 = (bf16[2048,256]{1,0:T(8,128)(2,1)}, bf16[2048,256]{1,0:T(8,128)(2,1)S(1)}, u32[]{:S(2)}, u32[]{:S(2)}) collective-permute-start(bf16[2048,256]{1,0:T(8,128)(2,1)} %get-tuple-element.12), channel_id=1, source_target_pairs={{0,1},{1,0},{2,3},{3,2},{4,5},{5,4},{6,7},{7,6},{8,9},{9,8},{10,11... | collective-permute-start | bytes 3145736 | tf_op jit(solution)/shard_map/ppermute | solution.py:221
  41.5 77.4 %collective-permute-start.3 = (bf16[2048,256]{1,0:T(8,128)(2,1)}, bf16[2048,256]{1,0:T(8,128)(2,1)}, u32[]{:S(2)}, u32[]{:S(2)}) collective-permute-start(bf16[2048,256]{1,0:T(8,128)(2,1)} %get-tuple-element.13), channel_id=1, source_target_pairs={{0,15},{1,2},{2,1},{3,4},{4,3},{5,6},{6,5},{7,8},{8,7},{9,10},{10,... | collective-permute-start | bytes 3145736 | tf_op jit(solution)/shard_map/ppermute | solution.py:222
  44.8 0.8 copy-start.3
  125.4 14.5 %copy-start.2 = (bf16[256,3712]{1,0:T(8,128)(2,1)}, bf16[256,3712]{1,0:T(8,128)(2,1)S(1)}, u32[]{:S(2)}) copy-start(bf16[256,3712]{1,0:T(8,128)(2,1)S(1)} %shard_map.95) | copy-start | bytes 5701636
  125.5 12.4 %collective-permute-start.5 = (bf16[32,1920]{1,0:T(8,128)(2,1)S(1)}, bf16[32,1920]{1,0:T(8,128)(2,1)S(1)}, u32[]{:S(2)}, u32[]{:S(2)}) collective-permute-start(bf16[32,1920]{1,0:T(8,128)(2,1)S(1)} %get-tuple-element.32), channel_id=1, source_target_pairs={{0,14},{1,15},{2,0},{3,1},{4,2},{5,3},{6,4},{7,5},{8,6},{9,7},{10,... | collective-permute-start | bytes 368648 | tf_op jit(solution)/shard_map/ppermute | solution.py:135
  130.3 7.6 %collective-permute-start.4 = (bf16[32,1792]{1,0:T(8,128)(2,1)S(1)}, bf16[32,1792]{1,0:T(8,128)(2,1)S(1)}, u32[]{:S(2)}, u32[]{:S(2)}) collective-permute-start(bf16[32,1792]{1,0:T(8,128)(2,1)S(1)} %get-tuple-element.31), channel_id=1, source_target_pairs={{0,2},{1,3},{2,4},{3,5},{4,6},{5,7},{6,8},{7,9},{8,10},{9,11},{10,... | collective-permute-start | bytes 344072 | tf_op jit(solution)/shard_map/ppermute | solution.py:134
  138.0 42.1 %copy-start.6 = (pred[64]{0:T(512)(128)(4,1)S(1)}, pred[64]{0:T(512)(128)(4,1)}, u32[]{:S(2)}) copy-start(pred[64]{0:T(512)(128)(4,1)} %get-tuple-element.34) | copy-start | bytes 196
  138.0 7.8 %collective-permute-start.7 = (bf16[32,3712]{1,0:T(8,128)(2,1)S(1)}, bf16[32,3712]{1,0:T(8,128)(2,1)S(1)}, u32[]{:S(2)}, u32[]{:S(2)}) collective-permute-start(bf16[32,3712]{1,0:T(8,128)(2,1)S(1)} %pad_maximum_fusion.5), channel_id=1, source_target_pairs={{0,14},{1,15},{2,0},{3,1},{4,2},{5,3},{6,4},{7,5},{8,6},{9,7},{10,... | collective-permute-start | bytes 712712 | tf_op jit(solution)/shard_map/ppermute | solution.py:145
  140.0 9.2 %collective-permute-start.6 = (bf16[32,3712]{1,0:T(8,128)(2,1)S(1)}, bf16[32,3712]{1,0:T(8,128)(2,1)S(1)}, u32[]{:S(2)}, u32[]{:S(2)}) collective-permute-start(bf16[32,3712]{1,0:T(8,128)(2,1)S(1)} %pad_maximum_fusion.4), channel_id=1, source_target_pairs={{0,2},{1,3},{2,4},{3,5},{4,6},{5,7},{6,8},{7,9},{8,10},{9,11},{10,... | collective-permute-start | bytes 712712 | tf_op jit(solution)/shard_map/ppermute | solution.py:144
  150.4 12.4 %collective-permute-start.8 = (bf16[32,3712]{1,0:T(8,128)(2,1)S(1)}, bf16[32,3712]{1,0:T(8,128)(2,1)S(1)}, u32[]{:S(2)}, u32[]{:S(2)}) collective-permute-start(bf16[32,3712]{1,0:T(8,128)(2,1)S(1)} %get-tuple-element.29), channel_id=1, source_target_pairs={{0,2},{1,3},{2,4},{3,5},{4,6},{5,7},{6,8},{7,9},{8,10},{9,11},{10,... | collective-permute-start | bytes 712712 | tf_op jit(solution)/shard_map/ppermute | solution.py:144
  153.5 9.3 %collective-permute-start.9 = (bf16[32,3712]{1,0:T(8,128)(2,1)S(1)}, bf16[32,3712]{1,0:T(8,128)(2,1)S(1)}, u32[]{:S(2)}, u32[]{:S(2)}) collective-permute-start(bf16[32,3712]{1,0:T(8,128)(2,1)S(1)} %get-tuple-element.28), channel_id=1, source_target_pairs={{0,14},{1,15},{2,0},{3,1},{4,2},{5,3},{6,4},{7,5},{8,6},{9,7},{10,... | collective-permute-start | bytes 712712 | tf_op jit(solution)/shard_map/ppermute | solution.py:145
  164.0 11.2 %collective-permute-start.10 = (bf16[32,3712]{1,0:T(8,128)(2,1)S(1)}, bf16[32,3712]{1,0:T(8,128)(2,1)S(1)}, u32[]{:S(2)}, u32[]{:S(2)}) collective-permute-start(bf16[32,3712]{1,0:T(8,128)(2,1)S(1)} %get-tuple-element.26), channel_id=1, source_target_pairs={{0,2},{1,3},{2,4},{3,5},{4,6},{5,7},{6,8},{7,9},{8,10},{9,11},{10,... | collective-permute-start | bytes 712712 | tf_op jit(solution)/shard_map/ppermute | solution.py:144
  168.0 12.0 %collective-permute-start.11 = (bf16[32,3712]{1,0:T(8,128)(2,1)S(1)}, bf16[32,3712]{1,0:T(8,128)(2,1)S(1)}, u32[]{:S(2)}, u32[]{:S(2)}) collective-permute-start(bf16[32,3712]{1,0:T(8,128)(2,1)S(1)} %get-tuple-element.27), channel_id=1, source_target_pairs={{0,14},{1,15},{2,0},{3,1},{4,2},{5,3},{6,4},{7,5},{8,6},{9,7},{10,... | collective-permute-start | bytes 712712 | tf_op jit(solution)/shard_map/ppermute | solution.py:145

commit v5 on v4

--- a/solution.py
+++ b/solution.py
@@ -163,6 +163,82 @@
     return scale, shift
 
 
+def send_kernel(rows_ref, ids_ref, weights_ref, out_ref, table_ref):
+    tokens, width = rows_ref.shape
+    groups = out_ref.shape[0]
+    rows = rows_ref[...]
+    scale, shift = power_scale(rows)
+    table_ref[:, :width] = jnp.concatenate([rows.astype(jnp.float32) * scale] * NODES_TOK, axis=0)
+    column = lax.broadcasted_iota(jnp.int32, (tokens, out_ref.shape[1] - width), 1)
+    group = lax.broadcasted_iota(jnp.int32, (tokens, groups), 1)
+    weights = weights_ref[...].astype(jnp.float32)
+    places = []
+    for pair in range(NODES_TOK):
+        one, two = 2 * pair, 2 * pair + 1
+        name = ids_ref[:, one : one + 1]
+        places.append(jnp.where(group == name // EXP_NODE, 1.0, 0.0))
+        even = name % EXP_NODE == 0
+        first, second = weights[:, one : one + 1], weights[:, two : two + 1]
+        table_ref[pair * tokens : (pair + 1) * tokens, width:] = (
+            jnp.where(column == 0, jnp.where(even, first, second), 0.0)
+            + jnp.where(column == 1, jnp.where(even, second, first), 0.0)
+            + jnp.where(column == EXP_NODE, shift, 0.0)
+        )
+    placed = jnp.concatenate(places, axis=0).astype(jnp.bfloat16)
+    out_ref[...] = lax.dot_general(
+        placed,
+        table_ref[...].astype(jnp.bfloat16),
+        (((0,), (0,)), ((), ())),
+        preferred_element_type=jnp.float32,
+    ).astype(jnp.bfloat16)
+
+
+def send_slots(rows, ids, weights, groups):
+    tokens, width = rows.shape
+    total = width + 2 * EXTRA
+    return pl.pallas_call(
+        send_kernel,
+        grid=(1,),
+        out_shape=jax.ShapeDtypeStruct((groups, total), jnp.bfloat16),
+        in_specs=[pl.BlockSpec(x.shape, lambda i: (0, 0)) for x in (rows, ids, weights)],
+        out_specs=pl.BlockSpec((groups, total), lambda i: (0, 0)),
+        scratch_shapes=[pltpu.VMEM((tokens * NODES_TOK, total), jnp.float32)],
+        compiler_params=pltpu.CompilerParams(vmem_limit_bytes=8 * 2**20),
+    )(rows, ids, weights)
+
+
+def compact_kernel(slots_ref, rows_ref, place_ref):
+    count, width = rows_ref.shape
+    slots = slots_ref.shape[0]
+    live = slots_ref[:, width - EXTRA : width - EXTRA + 1].astype(jnp.float32) > 0
+    live = jnp.where(live, 1.0, 0.0)
+    row = lax.broadcasted_iota(jnp.int32, (slots, slots), 0)
+    column = lax.broadcasted_iota(jnp.int32, (slots, slots), 1)
+    ahead = jnp.where(column < row, 1.0, 0.0).astype(jnp.bfloat16)
+    spread = jnp.broadcast_to(live, (slots, 128)).astype(jnp.bfloat16)
+    rank = jnp.dot(ahead, spread, preferred_element_type=jnp.float32)[:, :1]
+    index = lax.broadcasted_iota(jnp.int32, (slots, count), 1).astype(jnp.float32)
+    place = jnp.where((index == rank) & (live > 0), 1.0, 0.0).astype(jnp.bfloat16)
+    place_ref[...] = place
+    rows_ref[...] = lax.dot_general(
+        place, slots_ref[:, :width], (((0,), (0,)), ((), ())), preferred_element_type=jnp.float32
+    ).astype(jnp.bfloat16)
+
+
+def compact_slots(slots, count):
+    total, width = slots.shape
+    return pl.pallas_call(
+        compact_kernel,
+        out_shape=(
+            jax.ShapeDtypeStruct((count, width - EXTRA), jnp.bfloat16),
+            jax.ShapeDtypeStruct((total, count), jnp.bfloat16),
+        ),
+        in_specs=[pl.BlockSpec(memory_space=pltpu.VMEM)],
+        out_specs=[pl.BlockSpec(memory_space=pltpu.VMEM)] * 2,
+        compiler_params=pltpu.CompilerParams(vmem_limit_bytes=8 * 2**20),
+    )(slots)
+
+
 def exchange(x):
     return lax.all_to_all(x, "node", split_axis=0, concat_axis=0, tiled=True)
 
@@ -181,22 +257,8 @@
     placing = jnp.arange(node_count, dtype=jnp.int32)[:, None, None] == dest_node[None]
     pick = jnp.any(placing, axis=2).astype(jnp.bfloat16)
     hit = (pairs % EXP_NODE)[..., None] == jnp.arange(EXP_NODE, dtype=jnp.int32)
-    weights = gate_weights.reshape(tok_count, NODES_TOK, EXP_NODE, 1).astype(jnp.float32)
-    route_gate = jnp.sum(jnp.where(hit, weights, 0.0), axis=2)
-    send_gate = jnp.sum(jnp.where(placing[..., None], route_gate[None], 0.0), axis=(1, 2))
-    scale, shift = power_scale(output_gradient)
-    scaled = (output_gradient.astype(jnp.float32) * scale).astype(jnp.bfloat16)
-    send_rows = jnp.dot(pick, scaled, preferred_element_type=jnp.float32)
-    send_shift = jnp.dot(pick, shift.astype(jnp.bfloat16), preferred_element_type=jnp.float32)
-    send = jnp.concatenate(
-        [
-            send_rows.astype(jnp.bfloat16),
-            send_gate.astype(jnp.bfloat16),
-            send_shift.astype(jnp.bfloat16),
-            jnp.zeros((node_count, 2 * EXTRA - EXP_NODE - 1), jnp.bfloat16),
-        ],
-        axis=1,
-    ).reshape(node_count, 2, -1)
+    send = send_slots(output_gradient, expert_ids, gate_weights, node_count)
+    send = send.reshape(node_count, 2, -1)
 
     place = lax.axis_index("local")
     parity = lax.rem(place, 2)
@@ -206,6 +268,9 @@
     down = w_down[0]
     down_low = lax.ppermute(down, "local", low_pairs)
     down_high = lax.ppermute(down, "local", high_pairs)
+    send, w_gate, w_up, saved_gate, saved_up = lax.optimization_barrier(
+        (send, w_gate, w_up, saved_gate, saved_up)
+    )
     saved = jnp.concatenate([saved_gate, saved_up], axis=1)
     saved = saved.reshape(local_count // 2, 2, live_count, -1)
     mine, others = (
@@ -216,19 +281,12 @@
     )
     own = jnp.concatenate([w_gate[0], w_up[0]], axis=1)
     low, high = jnp.concatenate([own[:half], others]), jnp.concatenate([own[half:], others])
-    send, low, high = lax.optimization_barrier((send, low, high))
     slots = exchange(send).reshape(node_count, -1)
     low = lax.ppermute(low, "local", low_pairs)
     high = lax.ppermute(high, "local", high_pairs)
 
-    live = (slots[:, width] > 0).astype(jnp.int32)
-    rank = jnp.cumsum(live) - live
-    compact = (jnp.arange(live_count, dtype=jnp.int32)[:, None] == rank[None]) & (
-        live[None] > 0
-    )
-    compact = compact.astype(jnp.bfloat16)
-    rows = jnp.dot(compact, slots, preferred_element_type=jnp.float32)
-    rows = rows[:, : width + EXTRA].astype(jnp.float16)
+    rows, compact = compact_slots(slots, live_count)
+    rows = rows.astype(jnp.float16)
     rows = lax.all_gather(
         rows,
         "local",
@@ -253,7 +311,7 @@
     sums = ring_sum(parts, local_count // 2, 2, place // 2)
 
     back = lax.dot_general(
-        compact, sums, (((0,), (0,)), ((), ())), preferred_element_type=jnp.float32
+        compact, sums, (((1,), (0,)), ((), ())), preferred_element_type=jnp.float32
     ).astype(jnp.bfloat16)
     back = jnp.pad(back, ((0, 0), (0, EXTRA))).reshape(node_count, 2, -1)
     home = exchange(back).reshape(node_count, -1)

time: 221 us -> 218 us (0.986)
  blocking collectives: 106 us -> 71.1 us
  starting transfers between devices: 64.4 us -> 86 us
  waiting for transfers between devices: 24.2 us -> 39.2 us
  other arithmetic: 7.92 us -> 4.64 us
  matrix products: 4.24 us -> 2.02 us
    all_to_all x1 -> x0, blocking collectives: 36.7 us -> none  [exchange(): return lax.all_to_all(x, 'node', split_axis=0, concat_axis=0, tiled=True)]
    all_to_all x1 -> x2, starting transfers between devices: 18.2 us -> 40.4 us  [exchange(): return lax.all_to_all(x, 'node', split_axis=0, concat_axis=0, tiled=True)]
    all_to_all x1 -> x2, waiting for transfers between devices: 0.01 us -> 16.8 us  [exchange(): return lax.all_to_all(x, 'node', split_axis=0, concat_axis=0, tiled=True)]
    all_gather x1, blocking collectives: 68.9 us -> 71.1 us  [on_device(): lax.all_gather(rows, 'local', axis=0, tiled=True, axis_index_groups=[list...]
    dot_general x4 -> x1, matrix products: 3.45 us -> 1.23 us  [on_device(): lax.dot_general(compact, sums, (((1,), (0,)), ((), ())), preferred_elemen...]
  transfers between devices with their start and end apart: 13 -> 14, of which waited for: 6 -> 8; matrix products, arithmetic and copies ran while one was open for 2% -> 1% of each run, Pallas kernels for 0% -> 0%
where the time goes in v5:
time: 218 us
  starting transfers between devices  86 us (39%)
  blocking collectives  71.1 us (33%)
  waiting for transfers between devices  39.2 us (18%)
  Pallas kernels  7.13 us (3%)
  local copies, waits for them, and re-layouts  6.15 us (3%)
  other arithmetic  4.64 us (2%)
    all_gather x1, blocking collectives, on_device(): lax.all_gather(rows, 'local', axis=0, tiled=True, axis_index_groups=[list...  71.1 us
    all_to_all x2, starting transfers between devices, exchange(): return lax.all_to_all(x, 'node', split_axis=0, concat_axis=0, tiled=True)  40.4 us
    all_to_all x2, waiting for transfers between devices, exchange(): return lax.all_to_all(x, 'node', split_axis=0, concat_axis=0, tiled=True)  16.8 us
    ppermute x1, starting transfers between devices, on_device(): down_high = lax.ppermute(down, 'local', high_pairs)  11.6 us
    ppermute x3, starting transfers between devices, ring_sum(): one = lax.ppermute(one, 'local', right)  11.5 us
    ppermute x3, waiting for transfers between devices, ring_sum(): one = lax.ppermute(one, 'local', right)  10.3 us
    ppermute x3, starting transfers between devices, ring_sum(): two = lax.ppermute(two, 'local', left)  9.48 us
    ppermute x3, waiting for transfers between devices, ring_sum(): two = lax.ppermute(two, 'local', left)  7.05 us
  transfers between devices with their start and end apart: 14, of which 8 were waited for; matrix products, arithmetic and copies ran while one was open for 1% of the time, Pallas kernels for 0%

profile of v5, /device:TPU:1, one launch (start us, length us, event | category | flops | bytes accessed | tf_op | source)
XLA Modules:
  0.0 217.5 jit_solution(15251058987839097039)
XLA Ops:
  0.7 0.9 copy-done.4
  1.6 0.7 copy-done.5
  2.3 0.7 copy-done.7
  3.0 0.4 shard_map.95
  3.4 0.9 reshape.87
  4.3 18.2 %all-to-all-start = ((bf16[64,2,1920]{2,1,0:T(2,128)(2,1)}), bf16[64,2,1920]{2,1,0:T(2,128)(2,1)S(1)}, u32[]{:S(2)}, u32[]{:S(2)}) async-start(bf16[64,2,1920]{2,1,0:T(2,128)(2,1)} %reshape.87), calls=%async_computation | async-start | bytes 983040 | tf_op jit(solution)/shard_map/all_to_all | solution.py:243
  22.5 1.9 collective-permute-start
  24.5 11.6 %collective-permute-start.1 = (bf16[128,3584]{1,0:T(8,128)(2,1)}, bf16[128,3584]{1,0:T(8,128)(2,1)}, u32[]{:S(2)}, u32[]{:S(2)}) collective-permute-start(bf16[128,3584]{1,0:T(8,128)(2,1)} %bitcast.30), channel_id=1, source_target_pairs={{0,15},{1,2},{2,1},{3,4},{4,3},{5,6},{6,5},{7,8},{8,7},{9,10},{10,... | collective-permute-start | bytes 2752520 | tf_op jit(solution)/shard_map/ppermute | solution.py:270
  36.2 0.1 fusion
  36.3 1.5 pad_maximum_fusion
  37.8 1.9 collective-permute-start.2
  39.7 3.1 %collective-permute-start.3 = (bf16[2048,256]{1,0:T(8,128)(2,1)}, bf16[2048,256]{1,0:T(8,128)(2,1)}, u32[]{:S(2)}, u32[]{:S(2)}) collective-permute-start(bf16[2048,256]{1,0:T(8,128)(2,1)} %get-tuple-element.42), channel_id=1, source_target_pairs={{0,15},{1,2},{2,1},{3,4},{4,3},{5,6},{6,5},{7,8},{8,7},{9,10},{10,... | collective-permute-start | bytes 3145736 | tf_op jit(solution)/shard_map/ppermute | solution.py:286
  42.9 0.1 and_select_fusion.1.owner_ref
  43.0 0.0 all-to-all-done
  43.0 0.1 copy.27
  43.0 0.5 shard_map.96
  43.6 71.1 %all-gather.1 = f16[256,3712]{1,0:T(8,128)(2,1)S(1)} all-gather(f16[32,3712]{1,0:T(8,128)(2,1)S(1)} %convert_element_type.93), channel_id=1, replica_groups={{0,2,4,6,8,10,12,14},{1,3,5,7,9,11,13,15},{16,18,20,22,24,26,28,30},{17..., dimensions={0}, use_global_device_ids=true | all-gather | bytes 2138112 | tf_op jit(solution)/shard_map/all_gather | solution.py:290
  114.7 0.2 slice_convert_fusion.rows_ref
  115.0 0.9 copy-done.3
  115.9 6.2 %shard_map.97 = bf16[256,3712]{1,0:T(8,128)(2,1)S(1)} custom-call(s32[3]{0:T(128)S(1)} %and_select_fusion.1.owner_ref, f32[256,128]{1,0:T(8,128)S(1)} %slice_convert_fusion.1.extra_ref, bf16[256,3584]{1,0:T(8,128)(2,1)S(1)} %slice_convert_fusion.rows_ref, bf16[128,3584]{1,0:T(8,128)(2,1)S(1)} %bitcast.31, ...), custom_call_target="tpu_custom_call" | custom-call | flops 1644167168 | bytes 10092544 | tf_op jit(solution)/shard_map/pallas_call | solution.py:94
  122.2 3.5 %collective-permute-start.5 = (bf16[32,1920]{1,0:T(8,128)(2,1)S(1)}, bf16[32,1920]{1,0:T(8,128)(2,1)S(1)}, u32[]{:S(2)}, u32[]{:S(2)}) collective-permute-start(bf16[32,1920]{1,0:T(8,128)(2,1)S(1)} %get-tuple-element.38), channel_id=1, source_target_pairs={{0,14},{1,15},{2,0},{3,1},{4,2},{5,3},{6,4},{7,5},{8,6},{9,7},{10,... | collective-permute-start | bytes 368648 | tf_op jit(solution)/shard_map/ppermute | solution.py:135
  125.7 2.7 %collective-permute-start.4 = (bf16[32,1792]{1,0:T(8,128)(2,1)S(1)}, bf16[32,1792]{1,0:T(8,128)(2,1)S(1)}, u32[]{:S(2)}, u32[]{:S(2)}) collective-permute-start(bf16[32,1792]{1,0:T(8,128)(2,1)S(1)} %get-tuple-element.37), channel_id=1, source_target_pairs={{0,2},{1,3},{2,4},{3,5},{4,6},{5,7},{6,8},{7,9},{8,10},{9,11},{10,... | collective-permute-start | bytes 344072 | tf_op jit(solution)/shard_map/ppermute | solution.py:134
  128.4 5.0 %collective-permute-done.4 = bf16[32,1792]{1,0:T(8,128)(2,1)S(1)} collective-permute-done((bf16[32,1792]{1,0:T(8,128)(2,1)S(1)}, bf16[32,1792]{1,0:T(8,128)(2,1)S(1)}, u32[]{:S(2)}, u32[]{:S(2)}) %collective-permute-start.4) | collective-permute-done | bytes 114720 | tf_op jit(solution)/shard_map/ppermute | solution.py:134
  133.4 2.3 %collective-permute-start.7 = (bf16[32,3712]{1,0:T(8,128)(2,1)S(1)}, bf16[32,3712]{1,0:T(8,128)(2,1)S(1)}, u32[]{:S(2)}, u32[]{:S(2)}) collective-permute-start(bf16[32,3712]{1,0:T(8,128)(2,1)S(1)} %pad_maximum_fusion.5), channel_id=1, source_target_pairs={{0,14},{1,15},{2,0},{3,1},{4,2},{5,3},{6,4},{7,5},{8,6},{9,7},{10,... | collective-permute-start | bytes 712712 | tf_op jit(solution)/shard_map/ppermute | solution.py:145
  135.8 3.9 %collective-permute-start.6 = (bf16[32,3712]{1,0:T(8,128)(2,1)S(1)}, bf16[32,3712]{1,0:T(8,128)(2,1)S(1)}, u32[]{:S(2)}, u32[]{:S(2)}) collective-permute-start(bf16[32,3712]{1,0:T(8,128)(2,1)S(1)} %pad_maximum_fusion.4), channel_id=1, source_target_pairs={{0,2},{1,3},{2,4},{3,5},{4,6},{5,7},{6,8},{7,9},{8,10},{9,11},{10,... | collective-permute-start | bytes 712712 | tf_op jit(solution)/shard_map/ppermute | solution.py:144
  139.7 2.3 %collective-permute-done.7 = bf16[32,3712]{1,0:T(8,128)(2,1)S(1)} collective-permute-done((bf16[32,3712]{1,0:T(8,128)(2,1)S(1)}, bf16[32,3712]{1,0:T(8,128)(2,1)S(1)}, u32[]{:S(2)}, u32[]{:S(2)}) %collective-permute-start.7) | collective-permute-done | bytes 237600 | tf_op jit(solution)/shard_map/ppermute | solution.py:145
  142.1 2.8 %collective-permute-done.6 = bf16[32,3712]{1,0:T(8,128)(2,1)S(1)} collective-permute-done((bf16[32,3712]{1,0:T(8,128)(2,1)S(1)}, bf16[32,3712]{1,0:T(8,128)(2,1)S(1)}, u32[]{:S(2)}, u32[]{:S(2)}) %collective-permute-start.6) | collective-permute-done | bytes 237600 | tf_op jit(solution)/shard_map/ppermute | solution.py:144
  144.9 1.2 add_convert_fusion.3
  146.1 3.0 %collective-permute-start.8 = (bf16[32,3712]{1,0:T(8,128)(2,1)S(1)}, bf16[32,3712]{1,0:T(8,128)(2,1)S(1)}, u32[]{:S(2)}, u32[]{:S(2)}) collective-permute-start(bf16[32,3712]{1,0:T(8,128)(2,1)S(1)} %get-tuple-element.35), channel_id=1, source_target_pairs={{0,2},{1,3},{2,4},{3,5},{4,6},{5,7},{6,8},{7,9},{8,10},{9,11},{10,... | collective-permute-start | bytes 712712 | tf_op jit(solution)/shard_map/ppermute | solution.py:144
  149.1 4.4 %collective-permute-start.9 = (bf16[32,3712]{1,0:T(8,128)(2,1)S(1)}, bf16[32,3712]{1,0:T(8,128)(2,1)S(1)}, u32[]{:S(2)}, u32[]{:S(2)}) collective-permute-start(bf16[32,3712]{1,0:T(8,128)(2,1)S(1)} %get-tuple-element.34), channel_id=1, source_target_pairs={{0,14},{1,15},{2,0},{3,1},{4,2},{5,3},{6,4},{7,5},{8,6},{9,7},{10,... | collective-permute-start | bytes 712712 | tf_op jit(solution)/shard_map/ppermute | solution.py:145
  153.5 4.9 %collective-permute-done.8 = bf16[32,3712]{1,0:T(8,128)(2,1)S(1)} collective-permute-done((bf16[32,3712]{1,0:T(8,128)(2,1)S(1)}, bf16[32,3712]{1,0:T(8,128)(2,1)S(1)}, u32[]{:S(2)}, u32[]{:S(2)}) %collective-permute-start.8) | collective-permute-done | bytes 237600 | tf_op jit(solution)/shard_map/ppermute | solution.py:144
  158.4 2.0 collective-permute-done.9
  160.4 1.2 add_convert_fusion.2
  161.6 4.5 %collective-permute-start.10 = (bf16[32,3712]{1,0:T(8,128)(2,1)S(1)}, bf16[32,3712]{1,0:T(8,128)(2,1)S(1)}, u32[]{:S(2)}, u32[]{:S(2)}) collective-permute-start(bf16[32,3712]{1,0:T(8,128)(2,1)S(1)} %get-tuple-element.32), channel_id=1, source_target_pairs={{0,2},{1,3},{2,4},{3,5},{4,6},{5,7},{6,8},{7,9},{8,10},{9,11},{10,... | collective-permute-start | bytes 712712 | tf_op jit(solution)/shard_map/ppermute | solution.py:144
  166.1 2.9 %collective-permute-start.11 = (bf16[32,3712]{1,0:T(8,128)(2,1)S(1)}, bf16[32,3712]{1,0:T(8,128)(2,1)S(1)}, u32[]{:S(2)}, u32[]{:S(2)}) collective-permute-start(bf16[32,3712]{1,0:T(8,128)(2,1)S(1)} %get-tuple-element.33), channel_id=1, source_target_pairs={{0,14},{1,15},{2,0},{3,1},{4,2},{5,3},{6,4},{7,5},{8,6},{9,7},{10,... | collective-permute-start | bytes 712712 | tf_op jit(solution)/shard_map/ppermute | solution.py:145
  169.0 2.7 %collective-permute-done.10 = bf16[32,3712]{1,0:T(8,128)(2,1)S(1)} collective-permute-done((bf16[32,3712]{1,0:T(8,128)(2,1)S(1)}, bf16[32,3712]{1,0:T(8,128)(2,1)S(1)}, u32[]{:S(2)}, u32[]{:S(2)}) %collective-permute-start.10) | collective-permute-done | bytes 237600 | tf_op jit(solution)/shard_map/ppermute | solution.py:144
  171.7 2.7 %collective-permute-done.11 = bf16[32,3712]{1,0:T(8,128)(2,1)S(1)} collective-permute-done((bf16[32,3712]{1,0:T(8,128)(2,1)S(1)}, bf16[32,3712]{1,0:T(8,128)(2,1)S(1)}, u32[]{:S(2)}, u32[]{:S(2)}) %collective-permute-start.11) | collective-permute-done | bytes 237600 | tf_op jit(solution)/shard_map/ppermute | solution.py:145
  174.4 1.2 convolution_convert_fusion
  175.6 0.9 reshape.92
  176.5 22.1 %all-to-all-start.1 = ((bf16[64,2,1920]{2,1,0:T(2,128)(2,1)}), bf16[64,2,1920]{2,1,0:T(2,128)(2,1)S(1)}, u32[]{:S(2)}, u32[]{:S(2)}) async-start(bf16[64,2,1920]{2,1,0:T(2,128)(2,1)} %reshape.92), calls=%async_computation.1 | async-start | bytes 983040 | tf_op jit(solution)/shard_map/all_to_all | solution.py:243
  198.7 0.1 copy.16
  198.8 0.1 iota_compare_fusion
  198.9 16.8 %all-to-all-done.1 = bf16[64,2,1920]{2,1,0:T(2,128)(2,1)S(1)} async-done(((bf16[64,2,1920]{2,1,0:T(2,128)(2,1)}), bf16[64,2,1920]{2,1,0:T(2,128)(2,1)S(1)}, u32[]{:S(2)}, u32[]{:S(2)}) %all-to-all-start.1) | async-done | bytes 491552 | tf_op jit(solution)/shard_map/all_to_all | solution.py:243
  215.7 0.1 copy.28
  215.8 0.1 copy.26
  215.9 0.1 select_reduce_fusion
  216.1 0.7 copy.23
  216.7 0.8 convolution_convert_fusion.1
  (41 shorter events, 0.4 us)
Async XLA Ops:
  0.6 35.5 %copy-start.1 = (bf16[1,3584,128]{2,1,0:T(8,128)(2,1)S(1)}, bf16[1,3584,128]{2,1,0:T(8,128)(2,1)}, u32[]{:S(2)}) copy-start(bf16[1,3584,128]{2,1,0:T(8,128)(2,1)} %param.13) | copy-start | bytes 2752516
  0.6 35.5 %copy-start = (bf16[1,3584,128]{2,1,0:T(8,128)(2,1)S(1)}, bf16[1,3584,128]{2,1,0:T(8,128)(2,1)}, u32[]{:S(2)}) copy-start(bf16[1,3584,128]{2,1,0:T(8,128)(2,1)} %param.14) | copy-start | bytes 2752516
  0.7 1.0 copy-start.4
  1.6 0.7 copy-start.5
  2.3 0.7 copy-start.7
  3.0 33.1 %copy-start.8 = (bf16[512,128]{1,0:T(8,128)(2,1)S(1)}, bf16[512,128]{1,0:T(8,128)(2,1)}, u32[]{:S(2)}) copy-start(bf16[512,128]{1,0:T(8,128)(2,1)} %param.12) | copy-start | bytes 393220
  3.0 33.1 %copy-start.9 = (bf16[512,128]{1,0:T(8,128)(2,1)S(1)}, bf16[512,128]{1,0:T(8,128)(2,1)}, u32[]{:S(2)}) copy-start(bf16[512,128]{1,0:T(8,128)(2,1)} %param.11) | copy-start | bytes 393220
  4.3 38.7 %all-to-all-start = ((bf16[64,2,1920]{2,1,0:T(2,128)(2,1)}), bf16[64,2,1920]{2,1,0:T(2,128)(2,1)S(1)}, u32[]{:S(2)}, u32[]{:S(2)}) async-start(bf16[64,2,1920]{2,1,0:T(2,128)(2,1)} %reshape.87), calls=%async_computation | async-start | bytes 983040 | tf_op jit(solution)/shard_map/all_to_all | solution.py:243
  22.5 92.4 %collective-permute-start = (bf16[128,3584]{1,0:T(8,128)(2,1)}, bf16[128,3584]{1,0:T(8,128)(2,1)}, u32[]{:S(2)}, u32[]{:S(2)}) collective-permute-start(bf16[128,3584]{1,0:T(8,128)(2,1)} %bitcast.29), channel_id=1, source_target_pairs={{0,1},{1,0},{2,3},{3,2},{4,5},{5,4},{6,7},{7,6},{8,9},{9,8},{10,11... | collective-permute-start | bytes 2752520 | tf_op jit(solution)/shard_map/ppermute | solution.py:269
  24.5 90.5 %collective-permute-start.1 = (bf16[128,3584]{1,0:T(8,128)(2,1)}, bf16[128,3584]{1,0:T(8,128)(2,1)}, u32[]{:S(2)}, u32[]{:S(2)}) collective-permute-start(bf16[128,3584]{1,0:T(8,128)(2,1)} %bitcast.30), channel_id=1, source_target_pairs={{0,15},{1,2},{2,1},{3,4},{4,3},{5,6},{6,5},{7,8},{8,7},{9,10},{10,... | collective-permute-start | bytes 2752520 | tf_op jit(solution)/shard_map/ppermute | solution.py:270
  37.8 77.2 %collective-permute-start.2 = (bf16[2048,256]{1,0:T(8,128)(2,1)}, bf16[2048,256]{1,0:T(8,128)(2,1)S(1)}, u32[]{:S(2)}, u32[]{:S(2)}) collective-permute-start(bf16[2048,256]{1,0:T(8,128)(2,1)} %get-tuple-element.43), channel_id=1, source_target_pairs={{0,1},{1,0},{2,3},{3,2},{4,5},{5,4},{6,7},{7,6},{8,9},{9,8},{10,11... | collective-permute-start | bytes 3145736 | tf_op jit(solution)/shard_map/ppermute | solution.py:285
  39.7 75.3 %collective-permute-start.3 = (bf16[2048,256]{1,0:T(8,128)(2,1)}, bf16[2048,256]{1,0:T(8,128)(2,1)}, u32[]{:S(2)}, u32[]{:S(2)}) collective-permute-start(bf16[2048,256]{1,0:T(8,128)(2,1)} %get-tuple-element.42), channel_id=1, source_target_pairs={{0,15},{1,2},{2,1},{3,4},{4,3},{5,6},{6,5},{7,8},{8,7},{9,10},{10,... | collective-permute-start | bytes 3145736 | tf_op jit(solution)/shard_map/ppermute | solution.py:286
  114.7 1.2 copy-start.3
  122.1 13.6 %copy-start.2 = (bf16[256,3712]{1,0:T(8,128)(2,1)}, bf16[256,3712]{1,0:T(8,128)(2,1)S(1)}, u32[]{:S(2)}) copy-start(bf16[256,3712]{1,0:T(8,128)(2,1)S(1)} %shard_map.97) | copy-start | bytes 5701636
  122.2 11.2 %collective-permute-start.5 = (bf16[32,1920]{1,0:T(8,128)(2,1)S(1)}, bf16[32,1920]{1,0:T(8,128)(2,1)S(1)}, u32[]{:S(2)}, u32[]{:S(2)}) collective-permute-start(bf16[32,1920]{1,0:T(8,128)(2,1)S(1)} %get-tuple-element.38), channel_id=1, source_target_pairs={{0,14},{1,15},{2,0},{3,1},{4,2},{5,3},{6,4},{7,5},{8,6},{9,7},{10,... | collective-permute-start | bytes 368648 | tf_op jit(solution)/shard_map/ppermute | solution.py:135
  125.7 7.6 %collective-permute-start.4 = (bf16[32,1792]{1,0:T(8,128)(2,1)S(1)}, bf16[32,1792]{1,0:T(8,128)(2,1)S(1)}, u32[]{:S(2)}, u32[]{:S(2)}) collective-permute-start(bf16[32,1792]{1,0:T(8,128)(2,1)S(1)} %get-tuple-element.37), channel_id=1, source_target_pairs={{0,2},{1,3},{2,4},{3,5},{4,6},{5,7},{6,8},{7,9},{8,10},{9,11},{10,... | collective-permute-start | bytes 344072 | tf_op jit(solution)/shard_map/ppermute | solution.py:134
  133.4 8.6 %collective-permute-start.7 = (bf16[32,3712]{1,0:T(8,128)(2,1)S(1)}, bf16[32,3712]{1,0:T(8,128)(2,1)S(1)}, u32[]{:S(2)}, u32[]{:S(2)}) collective-permute-start(bf16[32,3712]{1,0:T(8,128)(2,1)S(1)} %pad_maximum_fusion.5), channel_id=1, source_target_pairs={{0,14},{1,15},{2,0},{3,1},{4,2},{5,3},{6,4},{7,5},{8,6},{9,7},{10,... | collective-permute-start | bytes 712712 | tf_op jit(solution)/shard_map/ppermute | solution.py:145
  135.8 9.1 %collective-permute-start.6 = (bf16[32,3712]{1,0:T(8,128)(2,1)S(1)}, bf16[32,3712]{1,0:T(8,128)(2,1)S(1)}, u32[]{:S(2)}, u32[]{:S(2)}) collective-permute-start(bf16[32,3712]{1,0:T(8,128)(2,1)S(1)} %pad_maximum_fusion.4), channel_id=1, source_target_pairs={{0,2},{1,3},{2,4},{3,5},{4,6},{5,7},{6,8},{7,9},{8,10},{9,11},{10,... | collective-permute-start | bytes 712712 | tf_op jit(solution)/shard_map/ppermute | solution.py:144
  146.1 12.3 %collective-permute-start.8 = (bf16[32,3712]{1,0:T(8,128)(2,1)S(1)}, bf16[32,3712]{1,0:T(8,128)(2,1)S(1)}, u32[]{:S(2)}, u32[]{:S(2)}) collective-permute-start(bf16[32,3712]{1,0:T(8,128)(2,1)S(1)} %get-tuple-element.35), channel_id=1, source_target_pairs={{0,2},{1,3},{2,4},{3,5},{4,6},{5,7},{6,8},{7,9},{8,10},{9,11},{10,... | collective-permute-start | bytes 712712 | tf_op jit(solution)/shard_map/ppermute | solution.py:144
  149.1 11.3 %collective-permute-start.9 = (bf16[32,3712]{1,0:T(8,128)(2,1)S(1)}, bf16[32,3712]{1,0:T(8,128)(2,1)S(1)}, u32[]{:S(2)}, u32[]{:S(2)}) collective-permute-start(bf16[32,3712]{1,0:T(8,128)(2,1)S(1)} %get-tuple-element.34), channel_id=1, source_target_pairs={{0,14},{1,15},{2,0},{3,1},{4,2},{5,3},{6,4},{7,5},{8,6},{9,7},{10,... | collective-permute-start | bytes 712712 | tf_op jit(solution)/shard_map/ppermute | solution.py:145
  161.6 10.1 %collective-permute-start.10 = (bf16[32,3712]{1,0:T(8,128)(2,1)S(1)}, bf16[32,3712]{1,0:T(8,128)(2,1)S(1)}, u32[]{:S(2)}, u32[]{:S(2)}) collective-permute-start(bf16[32,3712]{1,0:T(8,128)(2,1)S(1)} %get-tuple-element.32), channel_id=1, source_target_pairs={{0,2},{1,3},{2,4},{3,5},{4,6},{5,7},{6,8},{7,9},{8,10},{9,11},{10,... | collective-permute-start | bytes 712712 | tf_op jit(solution)/shard_map/ppermute | solution.py:144
  166.1 8.2 %collective-permute-start.11 = (bf16[32,3712]{1,0:T(8,128)(2,1)S(1)}, bf16[32,3712]{1,0:T(8,128)(2,1)S(1)}, u32[]{:S(2)}, u32[]{:S(2)}) collective-permute-start(bf16[32,3712]{1,0:T(8,128)(2,1)S(1)} %get-tuple-element.33), channel_id=1, source_target_pairs={{0,14},{1,15},{2,0},{3,1},{4,2},{5,3},{6,4},{7,5},{8,6},{9,7},{10,... | collective-permute-start | bytes 712712 | tf_op jit(solution)/shard_map/ppermute | solution.py:145
  174.4 24.3 %copy-start.6 = (s32[8,8]{1,0:T(8,128)S(1)}, s32[8,8]{1,0:T(8,128)}, u32[]{:S(2)}) copy-start(s32[8,8]{1,0:T(8,128)} %ids_ref.1) | copy-start | bytes 772
  176.5 39.2 %all-to-all-start.1 = ((bf16[64,2,1920]{2,1,0:T(2,128)(2,1)}), bf16[64,2,1920]{2,1,0:T(2,128)(2,1)S(1)}, u32[]{:S(2)}, u32[]{:S(2)}) async-start(bf16[64,2,1920]{2,1,0:T(2,128)(2,1)} %reshape.92), calls=%async_computation.1 | async-start | bytes 983040 | tf_op jit(solution)/shard_map/all_to_all | solution.py:243

commit v6 on v3

--- a/solution.py
+++ b/solution.py
@@ -159,6 +159,82 @@
     return scale, shift
 
 
+def send_kernel(rows_ref, ids_ref, weights_ref, out_ref, table_ref):
+    tokens, width = rows_ref.shape
+    groups = out_ref.shape[0]
+    rows = rows_ref[...]
+    scale, shift = power_scale(rows)
+    table_ref[:, :width] = jnp.concatenate([rows.astype(jnp.float32) * scale] * NODES_TOK, axis=0)
+    column = lax.broadcasted_iota(jnp.int32, (tokens, out_ref.shape[1] - width), 1)
+    group = lax.broadcasted_iota(jnp.int32, (tokens, groups), 1)
+    weights = weights_ref[...].astype(jnp.float32)
+    places = []
+    for pair in range(NODES_TOK):
+        one, two = 2 * pair, 2 * pair + 1
+        name = ids_ref[:, one : one + 1]
+        places.append(jnp.where(group == name // EXP_NODE, 1.0, 0.0))
+        even = name % EXP_NODE == 0
+        first, second = weights[:, one : one + 1], weights[:, two : two + 1]
+        table_ref[pair * tokens : (pair + 1) * tokens, width:] = (
+            jnp.where(column == 0, jnp.where(even, first, second), 0.0)
+            + jnp.where(column == 1, jnp.where(even, second, first), 0.0)
+            + jnp.where(column == EXP_NODE, shift, 0.0)
+        )
+    placed = jnp.concatenate(places, axis=0).astype(jnp.bfloat16)
+    out_ref[...] = lax.dot_general(
+        placed,
+        table_ref[...].astype(jnp.bfloat16),
+        (((0,), (0,)), ((), ())),
+        preferred_element_type=jnp.float32,
+    ).astype(jnp.bfloat16)
+
+
+def send_slots(rows, ids, weights, groups):
+    tokens, width = rows.shape
+    total = width + 2 * EXTRA
+    return pl.pallas_call(
+        send_kernel,
+        grid=(1,),
+        out_shape=jax.ShapeDtypeStruct((groups, total), jnp.bfloat16),
+        in_specs=[pl.BlockSpec(x.shape, lambda i: (0, 0)) for x in (rows, ids, weights)],
+        out_specs=pl.BlockSpec((groups, total), lambda i: (0, 0)),
+        scratch_shapes=[pltpu.VMEM((tokens * NODES_TOK, total), jnp.float32)],
+        compiler_params=pltpu.CompilerParams(vmem_limit_bytes=8 * 2**20),
+    )(rows, ids, weights)
+
+
+def compact_kernel(slots_ref, rows_ref, place_ref):
+    count, width = rows_ref.shape
+    slots = slots_ref.shape[0]
+    live = slots_ref[:, width - EXTRA : width - EXTRA + 1].astype(jnp.float32) > 0
+    live = jnp.where(live, 1.0, 0.0)
+    row = lax.broadcasted_iota(jnp.int32, (slots, slots), 0)
+    column = lax.broadcasted_iota(jnp.int32, (slots, slots), 1)
+    ahead = jnp.where(column < row, 1.0, 0.0).astype(jnp.bfloat16)
+    spread = jnp.broadcast_to(live, (slots, 128)).astype(jnp.bfloat16)
+    rank = jnp.dot(ahead, spread, preferred_element_type=jnp.float32)[:, :1]
+    index = lax.broadcasted_iota(jnp.int32, (slots, count), 1).astype(jnp.float32)
+    place = jnp.where((index == rank) & (live > 0), 1.0, 0.0).astype(jnp.bfloat16)
+    place_ref[...] = place
+    rows_ref[...] = lax.dot_general(
+        place, slots_ref[:, :width], (((0,), (0,)), ((), ())), preferred_element_type=jnp.float32
+    ).astype(jnp.bfloat16)
+
+
+def compact_slots(slots, count):
+    total, width = slots.shape
+    return pl.pallas_call(
+        compact_kernel,
+        out_shape=(
+            jax.ShapeDtypeStruct((count, width - EXTRA), jnp.bfloat16),
+            jax.ShapeDtypeStruct((total, count), jnp.bfloat16),
+        ),
+        in_specs=[pl.BlockSpec(memory_space=pltpu.VMEM)],
+        out_specs=[pl.BlockSpec(memory_space=pltpu.VMEM)] * 2,
+        compiler_params=pltpu.CompilerParams(vmem_limit_bytes=8 * 2**20),
+    )(slots)
+
+
 def exchange(x):
     return lax.all_to_all(x, "node", split_axis=0, concat_axis=0, tiled=True)
 
@@ -177,22 +253,8 @@
     placing = jnp.arange(node_count, dtype=jnp.int32)[:, None, None] == dest_node[None]
     pick = jnp.any(placing, axis=2).astype(jnp.bfloat16)
     hit = (pairs % EXP_NODE)[..., None] == jnp.arange(EXP_NODE, dtype=jnp.int32)
-    weights = gate_weights.reshape(tok_count, NODES_TOK, EXP_NODE, 1).astype(jnp.float32)
-    route_gate = jnp.sum(jnp.where(hit, weights, 0.0), axis=2)
-    send_gate = jnp.sum(jnp.where(placing[..., None], route_gate[None], 0.0), axis=(1, 2))
-    scale, shift = power_scale(output_gradient)
-    scaled = (output_gradient.astype(jnp.float32) * scale).astype(jnp.bfloat16)
-    send_rows = jnp.dot(pick, scaled, preferred_element_type=jnp.float32)
-    send_shift = jnp.dot(pick, shift.astype(jnp.bfloat16), preferred_element_type=jnp.float32)
-    send = jnp.concatenate(
-        [
-            send_rows.astype(jnp.bfloat16),
-            send_gate.astype(jnp.bfloat16),
-            send_shift.astype(jnp.bfloat16),
-            jnp.zeros((node_count, 2 * EXTRA - EXP_NODE - 1), jnp.bfloat16),
-        ],
-        axis=1,
-    ).reshape(node_count, 2, -1)
+    send = send_slots(output_gradient, expert_ids, gate_weights, node_count)
+    send = send.reshape(node_count, 2, -1)
 
     place = lax.axis_index("local")
     parity = lax.rem(place, 2)
@@ -205,14 +267,8 @@
     low = lax.ppermute(own[:half], "local", low_pairs)
     high = lax.ppermute(own[half:], "local", high_pairs)
 
-    live = (slots[:, width] > 0).astype(jnp.int32)
-    rank = jnp.cumsum(live) - live
-    compact = (jnp.arange(live_count, dtype=jnp.int32)[:, None] == rank[None]) & (
-        live[None] > 0
-    )
-    compact = compact.astype(jnp.bfloat16)
-    rows = jnp.dot(compact, slots, preferred_element_type=jnp.float32)
-    rows = rows[:, : width + EXTRA].astype(jnp.float16)
+    rows, compact = compact_slots(slots, live_count)
+    rows = rows.astype(jnp.float16)
     rows = lax.all_gather(rows, "local", axis=0, tiled=True)
 
     upward = lax.dot_general(
@@ -236,7 +292,7 @@
     sums = ring_sum(parts, local_count // 2, 2, place // 2)
 
     back = lax.dot_general(
-        compact, sums, (((0,), (0,)), ((), ())), preferred_element_type=jnp.float32
+        compact, sums, (((1,), (0,)), ((), ())), preferred_element_type=jnp.float32
     ).astype(jnp.bfloat16)
     back = jnp.pad(back, ((0, 0), (0, EXTRA))).reshape(node_count, 2, -1)
     home = exchange(back).reshape(node_count, -1)

time: 227 us -> 226 us (level)
  blocking collectives: 99.2 us -> 64.3 us
  starting transfers between devices: 65 us -> 85.3 us
  waiting for transfers between devices: 36.4 us -> 53.5 us
    all_to_all x1 -> x0, blocking collectives: 36.7 us -> none  [exchange(): return lax.all_to_all(x, 'node', split_axis=0, concat_axis=0, tiled=True)]
    all_to_all x1 -> x2, starting transfers between devices: 18.2 us -> 38.6 us  [exchange(): return lax.all_to_all(x, 'node', split_axis=0, concat_axis=0, tiled=True)]
    all_to_all x1 -> x2, waiting for transfers between devices: 2.16 us -> 19.1 us  [exchange(): return lax.all_to_all(x, 'node', split_axis=0, concat_axis=0, tiled=True)]
  transfers between devices with their start and end apart: 13 -> 14, of which waited for: 9 -> 10; matrix products, arithmetic and copies ran while one was open for 2% -> 1% of each run, Pallas kernels for 0% -> 1%
where the time goes in v6:
time: 226 us; the launch traced here: 224 us
  starting transfers between devices  85.3 us (38%)
  blocking collectives  64.3 us (28%)
  waiting for transfers between devices  53.5 us (24%)
  local copies, waits for them, and re-layouts  6.52 us (3%)
  Pallas kernels  5.61 us (2%)
  other arithmetic  4.47 us (2%)
  matrix products  3.13 us (1%)
    all_gather x1, blocking collectives, on_device(): rows = lax.all_gather(rows, 'local', axis=0, tiled=True)  64.3 us
    all_to_all x2, starting transfers between devices, exchange(): return lax.all_to_all(x, 'node', split_axis=0, concat_axis=0, tiled=True)  38.6 us
    ppermute x3, waiting for transfers between devices, ring_sum(): one = lax.ppermute(one, 'local', right)  20.2 us
    all_to_all x2, waiting for transfers between devices, exchange(): return lax.all_to_all(x, 'node', split_axis=0, concat_axis=0, tiled=True)  19.1 us
    ppermute x1, starting transfers between devices, on_device(): high = lax.ppermute(own[half:], 'local', high_pairs)  11.6 us
    ppermute x3, starting transfers between devices, ring_sum(): two = lax.ppermute(two, 'local', left)  11.1 us
    ppermute x3, starting transfers between devices, ring_sum(): one = lax.ppermute(one, 'local', right)  9.85 us
    ppermute x1, waiting for transfers between devices, on_device(): high_h = lax.ppermute(others, 'local', high_pairs)  4.58 us
  transfers between devices with their start and end apart: 14, of which 10 were waited for; matrix products, arithmetic and copies ran while one was open for 1% of the time, Pallas kernels for 1%

profile of v6, /device:TPU:1, one launch (start us, length us, event | category | flops | bytes accessed | tf_op | source)
XLA Modules:
  0.0 224.0 jit_solution(10821938645962270051)
XLA Ops:
  0.7 0.9 copy-done.4
  1.5 0.7 copy-done.5
  2.2 0.7 copy-done.7
  2.9 0.4 shard_map.95
  3.3 0.9 reshape.85
  4.2 1.7 pad_maximum_fusion.own_ref
  5.9 18.2 %all-to-all-start = ((bf16[64,2,1920]{2,1,0:T(2,128)(2,1)}), bf16[64,2,1920]{2,1,0:T(2,128)(2,1)S(1)}, u32[]{:S(2)}, u32[]{:S(2)}) async-start(bf16[64,2,1920]{2,1,0:T(2,128)(2,1)} %reshape.85), calls=%async_computation | async-start | bytes 983040 | tf_op jit(solution)/shard_map/all_to_all | solution.py:239
  24.1 1.4 fusion.10
  25.5 1.9 collective-permute-start.2
  27.4 11.6 %collective-permute-start.3 = (bf16[1792,256]{1,0:T(8,128)(2,1)}, bf16[1792,256]{1,0:T(8,128)(2,1)}, u32[]{:S(2)}, u32[]{:S(2)}) collective-permute-start(bf16[1792,256]{1,0:T(8,128)(2,1)} %get-tuple-element.38), channel_id=1, source_target_pairs={{0,15},{1,2},{2,1},{3,4},{4,3},{5,6},{6,5},{7,8},{8,7},{9,10},{10,... | collective-permute-start | bytes 2752520 | tf_op jit(solution)/shard_map/ppermute | solution.py:268
  39.0 0.1 pad_add_fusion.where_ref
  39.1 2.2 all-to-all-done
  41.3 0.1 copy.21
  41.3 0.5 shard_map.96
  41.9 64.3 %all-gather.1 = f16[512,3712]{1,0:T(8,128)(2,1)S(1)} all-gather(f16[32,3712]{1,0:T(8,128)(2,1)S(1)} %convert_element_type.93), channel_id=1, replica_groups=mesh['node'=64,'local'=16] {'local'}, dimensions={0}, use_global_device_ids=true | all-gather | bytes 4038656 | tf_op jit(solution)/shard_map/all_gather | solution.py:272
  106.3 1.1 fusion.up_ref
  107.4 1.0 shard_map.97
  108.4 4.1 %collective-permute-start = (bf16[8,32,384]{2,1,0:T(8,128)(2,1)S(1)}, bf16[8,32,384]{2,1,0:T(8,128)(2,1)S(1)}, u32[]{:S(2)}, u32[]{:S(2)}) collective-permute-start(bf16[8,32,384]{2,1,0:T(8,128)(2,1)S(1)} %get-tuple-element.18), channel_id=1, source_target_pairs={{0,1},{1,0},{2,3},{3,2},{4,5},{5,4},{6,7},{7,6},{8,9},{9,8},{10,11... | collective-permute-start | bytes 589832 | tf_op jit(solution)/shard_map/ppermute | solution.py:288
  112.5 2.0 collective-permute-start.1
  114.7 0.9 collective-permute-done
  115.6 4.6 %collective-permute-done.1 = bf16[8,32,384]{2,1,0:T(8,128)(2,1)S(1)} collective-permute-done((bf16[8,32,384]{2,1,0:T(8,128)(2,1)S(1)}, bf16[8,32,384]{2,1,0:T(8,128)(2,1)S(1)}, u32[]{:S(2)}, u32[]{:S(2)}) %collective-permute-start.1) | collective-permute-done | bytes 196640 | tf_op jit(solution)/shard_map/ppermute | solution.py:289
  120.2 3.7 %shard_map.98 = bf16[256,3712]{1,0:T(8,128)(2,1)S(1)} custom-call(bf16[256,384]{1,0:T(8,128)(2,1)S(1)} %bitcast.20, bf16[256,384]{1,0:T(8,128)(2,1)S(1)} %bitcast.21, bf16[256,384]{1,0:T(8,128)(2,1)S(1)} %bitcast.22, bf16[3584,256]{1,0:T(8,128)(2,1)S(1)} %pad_maximum_fusion.own_ref, bf16[1792,256]{1,0:T(8,128)(2,1)} %collective-permute-done.2.low_ref, ...), custom_call_target="tpu_custom_call" | custom-call | flops 939524096 | bytes 5505024 | tf_op jit(solution)/shard_map/pallas_call | solution.py:92
  123.9 1.9 collective-permute-start.5
  125.9 4.3 %collective-permute-start.4 = (bf16[32,1792]{1,0:T(8,128)(2,1)S(1)}, bf16[32,1792]{1,0:T(8,128)(2,1)S(1)}, u32[]{:S(2)}, u32[]{:S(2)}) collective-permute-start(bf16[32,1792]{1,0:T(8,128)(2,1)S(1)} %get-tuple-element.35), channel_id=1, source_target_pairs={{0,2},{1,3},{2,4},{3,5},{4,6},{5,7},{6,8},{7,9},{8,10},{9,11},{10,... | collective-permute-start | bytes 344072 | tf_op jit(solution)/shard_map/ppermute | solution.py:130
  130.1 4.4 %collective-permute-done.4 = bf16[32,1792]{1,0:T(8,128)(2,1)S(1)} collective-permute-done((bf16[32,1792]{1,0:T(8,128)(2,1)S(1)}, bf16[32,1792]{1,0:T(8,128)(2,1)S(1)}, u32[]{:S(2)}, u32[]{:S(2)}) %collective-permute-start.4) | collective-permute-done | bytes 114720 | tf_op jit(solution)/shard_map/ppermute | solution.py:130
  134.6 2.1 collective-permute-start.7
  136.7 4.1 %collective-permute-start.6 = (bf16[32,3712]{1,0:T(8,128)(2,1)S(1)}, bf16[32,3712]{1,0:T(8,128)(2,1)S(1)}, u32[]{:S(2)}, u32[]{:S(2)}) collective-permute-start(bf16[32,3712]{1,0:T(8,128)(2,1)S(1)} %pad_maximum_fusion.1), channel_id=1, source_target_pairs={{0,2},{1,3},{2,4},{3,5},{4,6},{5,7},{6,8},{7,9},{8,10},{9,11},{10,... | collective-permute-start | bytes 712712 | tf_op jit(solution)/shard_map/ppermute | solution.py:140
  140.9 2.4 %collective-permute-done.7 = bf16[32,3712]{1,0:T(8,128)(2,1)S(1)} collective-permute-done((bf16[32,3712]{1,0:T(8,128)(2,1)S(1)}, bf16[32,3712]{1,0:T(8,128)(2,1)S(1)}, u32[]{:S(2)}, u32[]{:S(2)}) %collective-permute-start.7) | collective-permute-done | bytes 237600 | tf_op jit(solution)/shard_map/ppermute | solution.py:141
  143.3 2.8 %collective-permute-done.6 = bf16[32,3712]{1,0:T(8,128)(2,1)S(1)} collective-permute-done((bf16[32,3712]{1,0:T(8,128)(2,1)S(1)}, bf16[32,3712]{1,0:T(8,128)(2,1)S(1)}, u32[]{:S(2)}, u32[]{:S(2)}) %collective-permute-start.6) | collective-permute-done | bytes 237600 | tf_op jit(solution)/shard_map/ppermute | solution.py:140
  146.1 1.2 add_convert_fusion.3
  147.3 3.3 %collective-permute-start.8 = (bf16[32,3712]{1,0:T(8,128)(2,1)S(1)}, bf16[32,3712]{1,0:T(8,128)(2,1)S(1)}, u32[]{:S(2)}, u32[]{:S(2)}) collective-permute-start(bf16[32,3712]{1,0:T(8,128)(2,1)S(1)} %get-tuple-element.33), channel_id=1, source_target_pairs={{0,2},{1,3},{2,4},{3,5},{4,6},{5,7},{6,8},{7,9},{8,10},{9,11},{10,... | collective-permute-start | bytes 712712 | tf_op jit(solution)/shard_map/ppermute | solution.py:140
  150.6 4.1 %collective-permute-start.9 = (bf16[32,3712]{1,0:T(8,128)(2,1)S(1)}, bf16[32,3712]{1,0:T(8,128)(2,1)S(1)}, u32[]{:S(2)}, u32[]{:S(2)}) collective-permute-start(bf16[32,3712]{1,0:T(8,128)(2,1)S(1)} %get-tuple-element.32), channel_id=1, source_target_pairs={{0,14},{1,15},{2,0},{3,1},{4,2},{5,3},{6,4},{7,5},{8,6},{9,7},{10,... | collective-permute-start | bytes 712712 | tf_op jit(solution)/shard_map/ppermute | solution.py:141
  154.7 8.8 %collective-permute-done.8 = bf16[32,3712]{1,0:T(8,128)(2,1)S(1)} collective-permute-done((bf16[32,3712]{1,0:T(8,128)(2,1)S(1)}, bf16[32,3712]{1,0:T(8,128)(2,1)S(1)}, u32[]{:S(2)}, u32[]{:S(2)}) %collective-permute-start.8) | collective-permute-done | bytes 237600 | tf_op jit(solution)/shard_map/ppermute | solution.py:140
  163.5 1.2 add_convert_fusion.2
  164.7 2.4 %collective-permute-start.10 = (bf16[32,3712]{1,0:T(8,128)(2,1)S(1)}, bf16[32,3712]{1,0:T(8,128)(2,1)S(1)}, u32[]{:S(2)}, u32[]{:S(2)}) collective-permute-start(bf16[32,3712]{1,0:T(8,128)(2,1)S(1)} %get-tuple-element.30), channel_id=1, source_target_pairs={{0,2},{1,3},{2,4},{3,5},{4,6},{5,7},{6,8},{7,9},{8,10},{9,11},{10,... | collective-permute-start | bytes 712712 | tf_op jit(solution)/shard_map/ppermute | solution.py:140
  167.1 4.9 %collective-permute-start.11 = (bf16[32,3712]{1,0:T(8,128)(2,1)S(1)}, bf16[32,3712]{1,0:T(8,128)(2,1)S(1)}, u32[]{:S(2)}, u32[]{:S(2)}) collective-permute-start(bf16[32,3712]{1,0:T(8,128)(2,1)S(1)} %get-tuple-element.31), channel_id=1, source_target_pairs={{0,14},{1,15},{2,0},{3,1},{4,2},{5,3},{6,4},{7,5},{8,6},{9,7},{10,... | collective-permute-start | bytes 712712 | tf_op jit(solution)/shard_map/ppermute | solution.py:141
  172.1 8.6 %collective-permute-done.10 = bf16[32,3712]{1,0:T(8,128)(2,1)S(1)} collective-permute-done((bf16[32,3712]{1,0:T(8,128)(2,1)S(1)}, bf16[32,3712]{1,0:T(8,128)(2,1)S(1)}, u32[]{:S(2)}, u32[]{:S(2)}) %collective-permute-start.10) | collective-permute-done | bytes 237600 | tf_op jit(solution)/shard_map/ppermute | solution.py:140
  180.7 1.9 collective-permute-done.11
  182.6 1.2 convolution_convert_fusion
  183.9 0.9 reshape.90
  184.8 20.3 %all-to-all-start.1 = ((bf16[64,2,1920]{2,1,0:T(2,128)(2,1)}), bf16[64,2,1920]{2,1,0:T(2,128)(2,1)S(1)}, u32[]{:S(2)}, u32[]{:S(2)}) async-start(bf16[64,2,1920]{2,1,0:T(2,128)(2,1)} %reshape.90), calls=%async_computation.1 | async-start | bytes 983040 | tf_op jit(solution)/shard_map/all_to_all | solution.py:239
  205.1 0.1 copy.14
  205.3 0.1 iota_compare_fusion
  205.3 17.0 %all-to-all-done.1 = bf16[64,2,1920]{2,1,0:T(2,128)(2,1)S(1)} async-done(((bf16[64,2,1920]{2,1,0:T(2,128)(2,1)}), bf16[64,2,1920]{2,1,0:T(2,128)(2,1)S(1)}, u32[]{:S(2)}, u32[]{:S(2)}) %all-to-all-start.1) | async-done | bytes 491552 | tf_op jit(solution)/shard_map/all_to_all | solution.py:239
  222.4 0.1 copy.20
  222.4 0.1 select_reduce_fusion
  222.6 0.7 copy.19
  223.2 0.8 convolution_convert_fusion.1
  (36 shorter events, 0.4 us)
Async XLA Ops:
  0.6 105.6 %copy-start = (bf16[1,128,3584]{2,1,0:T(8,128)(2,1)S(1)}, bf16[1,128,3584]{2,1,0:T(8,128)(2,1)}, u32[]{:S(2)}) copy-start(bf16[1,128,3584]{2,1,0:T(8,128)(2,1)} %param.15) | copy-start | bytes 2752516
  0.6 0.9 copy-start.4
  1.5 0.7 copy-start.5
  2.2 0.7 copy-start.7
  5.9 35.4 %all-to-all-start = ((bf16[64,2,1920]{2,1,0:T(2,128)(2,1)}), bf16[64,2,1920]{2,1,0:T(2,128)(2,1)S(1)}, u32[]{:S(2)}, u32[]{:S(2)}) async-start(bf16[64,2,1920]{2,1,0:T(2,128)(2,1)} %reshape.85), calls=%async_computation | async-start | bytes 983040 | tf_op jit(solution)/shard_map/all_to_all | solution.py:239
  25.5 89.1 %collective-permute-start.2 = (bf16[1792,256]{1,0:T(8,128)(2,1)}, bf16[1792,256]{1,0:T(8,128)(2,1)}, u32[]{:S(2)}, u32[]{:S(2)}) collective-permute-start(bf16[1792,256]{1,0:T(8,128)(2,1)} %get-tuple-element.39), channel_id=1, source_target_pairs={{0,1},{1,0},{2,3},{3,2},{4,5},{5,4},{6,7},{7,6},{8,9},{9,8},{10,11... | collective-permute-start | bytes 2752520 | tf_op jit(solution)/shard_map/ppermute | solution.py:267
  27.4 87.2 %collective-permute-start.3 = (bf16[1792,256]{1,0:T(8,128)(2,1)}, bf16[1792,256]{1,0:T(8,128)(2,1)}, u32[]{:S(2)}, u32[]{:S(2)}) collective-permute-start(bf16[1792,256]{1,0:T(8,128)(2,1)} %get-tuple-element.38), channel_id=1, source_target_pairs={{0,15},{1,2},{2,1},{3,4},{4,3},{5,6},{6,5},{7,8},{8,7},{9,10},{10,... | collective-permute-start | bytes 2752520 | tf_op jit(solution)/shard_map/ppermute | solution.py:268
  106.2 1.1 copy-start.2
  106.3 1.1 copy-start.3
  108.4 7.2 %collective-permute-start = (bf16[8,32,384]{2,1,0:T(8,128)(2,1)S(1)}, bf16[8,32,384]{2,1,0:T(8,128)(2,1)S(1)}, u32[]{:S(2)}, u32[]{:S(2)}) collective-permute-start(bf16[8,32,384]{2,1,0:T(8,128)(2,1)S(1)} %get-tuple-element.18), channel_id=1, source_target_pairs={{0,1},{1,0},{2,3},{3,2},{4,5},{5,4},{6,7},{7,6},{8,9},{9,8},{10,11... | collective-permute-start | bytes 589832 | tf_op jit(solution)/shard_map/ppermute | solution.py:288
  112.5 7.6 %collective-permute-start.1 = (bf16[8,32,384]{2,1,0:T(8,128)(2,1)S(1)}, bf16[8,32,384]{2,1,0:T(8,128)(2,1)S(1)}, u32[]{:S(2)}, u32[]{:S(2)}) collective-permute-start(bf16[8,32,384]{2,1,0:T(8,128)(2,1)S(1)} %get-tuple-element.18), channel_id=1, source_target_pairs={{0,15},{1,2},{2,1},{3,4},{4,3},{5,6},{6,5},{7,8},{8,7},{9,10},{10,... | collective-permute-start | bytes 589832 | tf_op jit(solution)/shard_map/ppermute | solution.py:289
  123.9 12.8 %copy-start.1 = (bf16[256,3712]{1,0:T(8,128)(2,1)}, bf16[256,3712]{1,0:T(8,128)(2,1)S(1)}, u32[]{:S(2)}) copy-start(bf16[256,3712]{1,0:T(8,128)(2,1)S(1)} %shard_map.98) | copy-start | bytes 5701636
  123.9 10.6 %collective-permute-start.5 = (bf16[32,1920]{1,0:T(8,128)(2,1)S(1)}, bf16[32,1920]{1,0:T(8,128)(2,1)S(1)}, u32[]{:S(2)}, u32[]{:S(2)}) collective-permute-start(bf16[32,1920]{1,0:T(8,128)(2,1)S(1)} %get-tuple-element.36), channel_id=1, source_target_pairs={{0,14},{1,15},{2,0},{3,1},{4,2},{5,3},{6,4},{7,5},{8,6},{9,7},{10,... | collective-permute-start | bytes 368648 | tf_op jit(solution)/shard_map/ppermute | solution.py:131
  125.9 8.6 %collective-permute-start.4 = (bf16[32,1792]{1,0:T(8,128)(2,1)S(1)}, bf16[32,1792]{1,0:T(8,128)(2,1)S(1)}, u32[]{:S(2)}, u32[]{:S(2)}) collective-permute-start(bf16[32,1792]{1,0:T(8,128)(2,1)S(1)} %get-tuple-element.35), channel_id=1, source_target_pairs={{0,2},{1,3},{2,4},{3,5},{4,6},{5,7},{6,8},{7,9},{8,10},{9,11},{10,... | collective-permute-start | bytes 344072 | tf_op jit(solution)/shard_map/ppermute | solution.py:130
  134.6 8.7 %collective-permute-start.7 = (bf16[32,3712]{1,0:T(8,128)(2,1)S(1)}, bf16[32,3712]{1,0:T(8,128)(2,1)S(1)}, u32[]{:S(2)}, u32[]{:S(2)}) collective-permute-start(bf16[32,3712]{1,0:T(8,128)(2,1)S(1)} %pad_maximum_fusion.2), channel_id=1, source_target_pairs={{0,14},{1,15},{2,0},{3,1},{4,2},{5,3},{6,4},{7,5},{8,6},{9,7},{10,... | collective-permute-start | bytes 712712 | tf_op jit(solution)/shard_map/ppermute | solution.py:141
  136.7 9.3 %collective-permute-start.6 = (bf16[32,3712]{1,0:T(8,128)(2,1)S(1)}, bf16[32,3712]{1,0:T(8,128)(2,1)S(1)}, u32[]{:S(2)}, u32[]{:S(2)}) collective-permute-start(bf16[32,3712]{1,0:T(8,128)(2,1)S(1)} %pad_maximum_fusion.1), channel_id=1, source_target_pairs={{0,2},{1,3},{2,4},{3,5},{4,6},{5,7},{6,8},{7,9},{8,10},{9,11},{10,... | collective-permute-start | bytes 712712 | tf_op jit(solution)/shard_map/ppermute | solution.py:140
  147.3 16.2 %collective-permute-start.8 = (bf16[32,3712]{1,0:T(8,128)(2,1)S(1)}, bf16[32,3712]{1,0:T(8,128)(2,1)S(1)}, u32[]{:S(2)}, u32[]{:S(2)}) collective-permute-start(bf16[32,3712]{1,0:T(8,128)(2,1)S(1)} %get-tuple-element.33), channel_id=1, source_target_pairs={{0,2},{1,3},{2,4},{3,5},{4,6},{5,7},{6,8},{7,9},{8,10},{9,11},{10,... | collective-permute-start | bytes 712712 | tf_op jit(solution)/shard_map/ppermute | solution.py:140
  150.6 12.9 %collective-permute-start.9 = (bf16[32,3712]{1,0:T(8,128)(2,1)S(1)}, bf16[32,3712]{1,0:T(8,128)(2,1)S(1)}, u32[]{:S(2)}, u32[]{:S(2)}) collective-permute-start(bf16[32,3712]{1,0:T(8,128)(2,1)S(1)} %get-tuple-element.32), channel_id=1, source_target_pairs={{0,14},{1,15},{2,0},{3,1},{4,2},{5,3},{6,4},{7,5},{8,6},{9,7},{10,... | collective-permute-start | bytes 712712 | tf_op jit(solution)/shard_map/ppermute | solution.py:141
  164.7 16.0 %collective-permute-start.10 = (bf16[32,3712]{1,0:T(8,128)(2,1)S(1)}, bf16[32,3712]{1,0:T(8,128)(2,1)S(1)}, u32[]{:S(2)}, u32[]{:S(2)}) collective-permute-start(bf16[32,3712]{1,0:T(8,128)(2,1)S(1)} %get-tuple-element.30), channel_id=1, source_target_pairs={{0,2},{1,3},{2,4},{3,5},{4,6},{5,7},{6,8},{7,9},{8,10},{9,11},{10,... | collective-permute-start | bytes 712712 | tf_op jit(solution)/shard_map/ppermute | solution.py:140
  167.1 15.5 %collective-permute-start.11 = (bf16[32,3712]{1,0:T(8,128)(2,1)S(1)}, bf16[32,3712]{1,0:T(8,128)(2,1)S(1)}, u32[]{:S(2)}, u32[]{:S(2)}) collective-permute-start(bf16[32,3712]{1,0:T(8,128)(2,1)S(1)} %get-tuple-element.31), channel_id=1, source_target_pairs={{0,14},{1,15},{2,0},{3,1},{4,2},{5,3},{6,4},{7,5},{8,6},{9,7},{10,... | collective-permute-start | bytes 712712 | tf_op jit(solution)/shard_map/ppermute | solution.py:141
  182.6 22.5 %copy-start.6 = (s32[8,8]{1,0:T(8,128)S(1)}, s32[8,8]{1,0:T(8,128)}, u32[]{:S(2)}) copy-start(s32[8,8]{1,0:T(8,128)} %ids_ref.1) | copy-start | bytes 772
  184.8 37.5 %all-to-all-start.1 = ((bf16[64,2,1920]{2,1,0:T(2,128)(2,1)}), bf16[64,2,1920]{2,1,0:T(2,128)(2,1)S(1)}, u32[]{:S(2)}, u32[]{:S(2)}) async-start(bf16[64,2,1920]{2,1,0:T(2,128)(2,1)} %reshape.90), calls=%async_computation.1 | async-start | bytes 983040 | tf_op jit(solution)/shard_map/all_to_all | solution.py:239
